TPU v7x, 32 devices: a whole 2x2x4 slice. The times are simulated.
32 devices in a mesh: dp: 2 (over x), expert: 16 (over z, y, core).
Axes of the slice: x: 2, y: 2, z: 4, core: 2. Of those that a mesh axis runs over, the one named last changes fastest.
Arguments:
- tokens: bfloat16 [1792, 2048], P(('dp', 'expert')), may hold values from -6 to 6
- expert_ids: int32 [1792, 8], P(('dp', 'expert')), may hold values from 0 to 15, all different within a row; in each aligned block of 56 rows (0 to 55, 56 to 111, ...) at most 32 rows name the same one
- combine: float32 [1792, 8], P(('dp', 'expert')), may hold values from 0.2 to 1
- w_gate: bfloat16 [16, 2048, 768], P('expert'), may hold values from -0.125 to 0.125
- w_up: bfloat16 [16, 2048, 768], P('expert'), may hold values from -0.125 to 0.125
- w_down: bfloat16 [16, 768, 2048], P('expert'), may hold values from -0.21875 to 0.21875
- grad_out: bfloat16 [1792, 2048], P(('dp', 'expert')), may hold values from -6 to 6
Outputs:
- mixed: bfloat16 [1792, 2048], P(('dp', 'expert'))
- grad_tokens: bfloat16 [1792, 2048], P(('dp', 'expert'))
- grad_gate: bfloat16 [16, 2048, 768], P('expert', 'dp')
- grad_up: bfloat16 [16, 2048, 768], P('expert', 'dp')
- grad_down: bfloat16 [16, 768, 2048], P('expert', None, 'dp')
Inputs may be any that keep to these rules, and one draw needn't show every extreme that they name: `expert_ids`: each row names 8 different experts. Within the 56 rows of one device no expert is named by more than 32 rows, and in every draw some expert is named by exactly 32 rows of some device.
All inputs are finite; a program needn't handle non-finite values.
Results may differ from a plain program's by a relative error of at most 0.017.
Values may be sent and summed in bfloat16 or wider, within the bound.
A program may use at most 128 MiB of HBM per device.

v0:
```python
import jax
import jax.numpy as jnp
from jax import lax
from jax.sharding import PartitionSpec as P


def activations(rows, w_gate, w_up):
    gate = jnp.dot(rows, w_gate, preferred_element_type=jnp.float32)
    upper = jnp.dot(rows, w_up, preferred_element_type=jnp.float32)
    sigma = jax.nn.sigmoid(gate)
    hidden = (gate * sigma * upper).astype(jnp.bfloat16)
    return (gate, upper, sigma, hidden)


def expert_backward(rows, cotangent, gate, upper, sigma, hidden, w_gate, w_up, w_down):
    d_hidden = lax.dot_general(
        cotangent, w_down, (((1,), (1,)), ((), ())), preferred_element_type=jnp.float32
    )
    d_gate = (d_hidden * upper * sigma * (1.0 + gate * (1.0 - sigma))).astype(jnp.bfloat16)
    d_upper = (d_hidden * gate * sigma).astype(jnp.bfloat16)
    d_rows = lax.dot_general(
        d_gate, w_gate, (((1,), (1,)), ((), ())), preferred_element_type=jnp.float32
    )
    d_rows = (
        d_rows
        + lax.dot_general(
            d_upper, w_up, (((1,), (1,)), ((), ())), preferred_element_type=jnp.float32
        )
    ).astype(jnp.bfloat16)
    grad_g = lax.dot_general(
        rows, d_gate, (((0,), (0,)), ((), ())), preferred_element_type=jnp.float32
    ).astype(jnp.bfloat16)
    grad_u = lax.dot_general(
        rows, d_upper, (((0,), (0,)), ((), ())), preferred_element_type=jnp.float32
    ).astype(jnp.bfloat16)
    grad_d = lax.dot_general(
        hidden, cotangent, (((0,), (0,)), ((), ())), preferred_element_type=jnp.float32
    ).astype(jnp.bfloat16)
    return (d_rows, grad_g, grad_u, grad_d)


def on_device(tokens, expert_ids, combine, w_gate, w_up, w_down, grad_out):
    n_experts = lax.axis_size("expert")
    tok_rows, width = tokens.shape
    chosen = expert_ids.shape[1]
    capacity = min(tok_rows, tok_rows * chosen * 8 // (n_experts * 7))
    n_slots = n_experts * capacity
    flat = expert_ids.reshape(-1)
    onehot = (flat[:, None] == jnp.arange(n_experts, dtype=jnp.int32)[None, :]).astype(jnp.int32)
    ranks = jnp.sum(jnp.cumsum(onehot, axis=0) * onehot, axis=1) - 1
    target = flat * capacity + ranks
    match = jnp.arange(n_slots, dtype=jnp.int32)[:, None] == target[None, :]
    assign_table = match.astype(jnp.bfloat16)
    match_tok = match.reshape(n_slots, tok_rows, chosen)
    token_table = jnp.any(match_tok, axis=2).astype(jnp.bfloat16)
    weight_table = jnp.sum(jnp.where(match_tok, combine[None, :, :], 0.0), axis=2)
    weight_g = w_gate[0]
    weight_u = w_up[0]
    weight_d = w_down[0]
    x_slots = (
        jnp.dot(token_table, tokens, preferred_element_type=jnp.float32)
        .astype(jnp.bfloat16)
        .reshape(n_experts, capacity, width)
    )
    cot_rows = (
        (combine[:, :, None] * grad_out[:, None, :].astype(jnp.float32))
        .astype(jnp.bfloat16)
        .reshape(tok_rows * chosen, width)
    )
    recv_x = lax.all_to_all(x_slots, "expert", split_axis=0, concat_axis=0, tiled=True)
    rows = recv_x.reshape(n_slots, width)
    gate, upper, sigma, hidden = activations(rows, weight_g, weight_u)
    out_slots = (
        jnp.dot(hidden, weight_d, preferred_element_type=jnp.float32)
        .astype(jnp.bfloat16)
        .reshape(n_experts, capacity, width)
    )
    back = lax.all_to_all(out_slots, "expert", split_axis=0, concat_axis=0, tiled=True)
    mixed = lax.dot_general(
        weight_table,
        back.reshape(n_slots, width).astype(jnp.float32),
        (((0,), (0,)), ((), ())),
        precision=lax.Precision.HIGHEST,
        preferred_element_type=jnp.float32,
    ).astype(jnp.bfloat16)
    cotangent = lax.all_to_all(
        jnp.dot(assign_table, cot_rows, preferred_element_type=jnp.float32)
        .astype(jnp.bfloat16)
        .reshape(n_experts, capacity, width),
        "expert",
        split_axis=0,
        concat_axis=0,
        tiled=True,
    ).reshape(n_slots, width)
    d_rows, grad_g, grad_u, grad_d = expert_backward(
        rows, cotangent, gate, upper, sigma, hidden, weight_g, weight_u, weight_d
    )
    d_slots = d_rows.reshape(n_experts, capacity, width)
    d_back = lax.all_to_all(d_slots, "expert", split_axis=0, concat_axis=0, tiled=True)
    grad_tokens = lax.dot_general(
        token_table,
        d_back.reshape(n_slots, width),
        (((0,), (0,)), ((), ())),
        preferred_element_type=jnp.float32,
    ).astype(jnp.bfloat16)
    sum_g, sum_u, sum_d = (
        lax.psum_scatter(grad_g[None], "dp", scatter_dimension=1, tiled=True).astype(jnp.float32),
        lax.psum_scatter(grad_u[None], "dp", scatter_dimension=1, tiled=True).astype(jnp.float32),
        lax.psum_scatter(grad_d[None], "dp", scatter_dimension=2, tiled=True).astype(jnp.float32),
    )
    return (
        mixed,
        grad_tokens,
        sum_g.astype(jnp.bfloat16),
        sum_u.astype(jnp.bfloat16),
        sum_d.astype(jnp.bfloat16),
    )


def solution(mesh):
    in_specs = (
        P(("dp", "expert"), None),
        P(("dp", "expert"), None),
        P(("dp", "expert"), None),
        P("expert", None, None),
        P("expert", None, None),
        P("expert", None, None),
        P(("dp", "expert"), None),
    )
    out_specs = (
        P(("dp", "expert"), None),
        P(("dp", "expert"), None),
        P("expert", "dp", None),
        P("expert", "dp", None),
        P("expert", None, "dp"),
    )
    return jax.shard_map(
        on_device, mesh=mesh, in_specs=in_specs, out_specs=out_specs, check_vma=False
    )
```

profile of v0, /device:TPU:14, one launch (start us, length us, event | category | flops | bytes accessed | tf_op | source)
XLA Modules:
  0.0 277.6 jit_solution(5856246886597833111)
XLA Ops:
  7.2 0.9 copy.33
  8.1 0.1 mul.67
  8.2 0.8 copy.28
  9.1 1.2 reduce-window.6
  10.2 0.2 slice_reduce_fusion
  10.6 1.0 convert_element_type.59
  11.6 2.7 convolution_convert_fusion.3
  14.3 6.4 %all-to-all-start.2 = ((bf16[16,32,2048]{2,1,0:T(8,128)(2,1)}), bf16[16,32,2048]{2,1,0:T(8,128)(2,1)}, u32[]{:S(2)}, u32[]{:S(2)}) async-start(bf16[16,32,2048]{2,1,0:T(8,128)(2,1)} %bitcast.72), calls=%async_computation.2 | async-start | bytes 4194304 | tf_op jit(solution)/shard_map/all_to_all | solution.py:86
  20.9 0.4 fusion.24
  21.3 3.1 %convolution_convert_fusion.4 = bf16[512,2048]{1,0:T(8,128)(2,1)} fusion(pred[512,56]{0,1:T(8,128)(4,1)S(1)} %fusion.24, bf16[56,2048]{1,0:T(8,128)(2,1)} %param.7), kind=kOutput, calls=%fused_computation.20 | convolution fusion | flops 118489088 | bytes 2355200 | tf_op jit(solution)/shard_map/dot_general | solution.py:61
  24.4 43.7 %all-to-all-done.2 = bf16[16,32,2048]{2,1,0:T(8,128)(2,1)} async-done(((bf16[16,32,2048]{2,1,0:T(8,128)(2,1)}), bf16[16,32,2048]{2,1,0:T(8,128)(2,1)}, u32[]{:S(2)}, u32[]{:S(2)}) %all-to-all-start.2) | async-done | bytes 2097184 | tf_op jit(solution)/shard_map/all_to_all | solution.py:86
  68.1 5.1 %all-to-all-start = ((bf16[16,32,2048]{2,1,0:T(8,128)(2,1)}), bf16[16,32,2048]{2,1,0:T(8,128)(2,1)}, u32[]{:S(2)}, u32[]{:S(2)}) async-start(bf16[16,32,2048]{2,1,0:T(8,128)(2,1)} %bitcast.70), calls=%async_computation | async-start | bytes 4194304 | tf_op jit(solution)/shard_map/all_to_all | solution.py:70
  73.2 5.5 %fusion.1 = f32[512,768]{1,0:T(8,128)} fusion(bf16[512,2048]{1,0:T(8,128)(2,1)} %bitcast.10, bf16[1,768,2048]{2,1,0:T(8,128)(2,1)} %param.12), kind=kOutput, calls=%fused_computation.6 | convolution fusion | flops 1610612736 | bytes 6815744 | tf_op jit(solution)/shard_map/dot_general | solution.py:16
  78.7 41.8 %all-to-all-done = bf16[16,32,2048]{2,1,0:T(8,128)(2,1)} async-done(((bf16[16,32,2048]{2,1,0:T(8,128)(2,1)}), bf16[16,32,2048]{2,1,0:T(8,128)(2,1)}, u32[]{:S(2)}, u32[]{:S(2)}) %all-to-all-start) | async-done | bytes 2097184 | tf_op jit(solution)/shard_map/all_to_all | solution.py:70
  120.5 4.4 %fusion.7 = f32[512,768]{1,0:T(8,128)S(1)} fusion(bf16[512,2048]{1,0:T(8,128)(2,1)} %bitcast.2, bf16[1,2048,768]{2,1,0:T(8,128)(2,1)} %param.11), kind=kOutput, calls=%fused_computation.12 | convolution fusion | flops 1610612736 | bytes 6815744 | tf_op jit(solution)/shard_map/dot_general | solution.py:9
  125.0 5.1 %multiply_convert_fusion.1 = (bf16[512,768]{1,0:T(8,128)(2,1)}, bf16[512,768]{1,0:T(8,128)(2,1)S(1)}, bf16[512,768]{1,0:T(8,128)(2,1)}) fusion(f32[512,768]{1,0:T(8,128)S(1)} %copy-done.4, f32[512,768]{1,0:T(8,128)S(1)} %fusion.7, bf16[512,2048]{1,0:T(8,128)(2,1)} %bitcast.2, bf16[1,2048,768]{2,1,0:T(8,128)(2,1)S(1)} %copy-done), kind=kOutput, calls=%fused_computation.29 | convolution fusion | flops 1616904192 | bytes 10747904 | tf_op jit(solution)/shard_map/dot_general | solution.py:8
  130.0 0.9 copy-done.3
  131.0 5.1 %fusion.18 = bf16[1,768,2048]{2,1,0:T(8,128)(2,1)} fusion(bf16[512,768]{1,0:T(8,128)(2,1)S(1)} %get-tuple-element.6, bf16[512,2048]{1,0:T(8,128)(2,1)} %bitcast.10), kind=kOutput, calls=%fused_computation.23 | convolution fusion | flops 1612185600 | bytes 6029312 | tf_op jit(solution)/shard_map/dot_general | solution.py:36
  136.1 0.2 reduce-scatter.4.cloned.1.call-start
  136.3 5.3 %fusion.16 = bf16[1,2048,768]{2,1,0:T(8,128)(2,1)} fusion(bf16[512,2048]{1,0:T(8,128)(2,1)} %bitcast.2, bf16[512,768]{1,0:T(8,128)(2,1)} %get-tuple-element.5), kind=kOutput, calls=%fused_computation.21 | convolution fusion | flops 1612185600 | bytes 6029312 | tf_op jit(solution)/shard_map/dot_general | solution.py:30
  141.6 4.9 %fusion.5 = f32[512,2048]{1,0:T(8,128)S(1)} fusion(bf16[512,768]{1,0:T(8,128)(2,1)} %get-tuple-element.7, bf16[1,2048,768]{2,1,0:T(8,128)(2,1)} %param.11), kind=kOutput, calls=%fused_computation.10 | convolution fusion | flops 1610612736 | bytes 8126464 | tf_op jit(solution)/shard_map/dot_general | solution.py:26
  146.6 3.1 %add_convert_fusion = bf16[512,2048]{1,0:T(8,128)(2,1)} fusion(f32[512,2048]{1,0:T(8,128)S(1)} %fusion.5, bf16[512,768]{1,0:T(8,128)(2,1)S(1)} %copy-done.2, bf16[1,2048,768]{2,1,0:T(8,128)(2,1)S(1)} %copy-done), kind=kOutput, calls=%fused_computation | convolution fusion | flops 1612709888 | bytes 10223616 | tf_op jit(solution)/shard_map/dot_general | solution.py:21
  149.7 4.6 %all-to-all-start.3 = ((bf16[16,32,2048]{2,1,0:T(8,128)(2,1)}), bf16[16,32,2048]{2,1,0:T(8,128)(2,1)}, u32[]{:S(2)}, u32[]{:S(2)}) async-start(bf16[16,32,2048]{2,1,0:T(8,128)(2,1)} %bitcast.71), calls=%async_computation.3 | async-start | bytes 4194304 | tf_op jit(solution)/shard_map/all_to_all | solution.py:99
  154.4 5.3 %fusion.17 = bf16[1,2048,768]{2,1,0:T(8,128)(2,1)} fusion(bf16[512,2048]{1,0:T(8,128)(2,1)} %bitcast.2, bf16[512,768]{1,0:T(8,128)(2,1)} %get-tuple-element.7), kind=kOutput, calls=%fused_computation.22 | convolution fusion | flops 1612185600 | bytes 6029312 | tf_op jit(solution)/shard_map/dot_general | solution.py:33
  159.7 5.3 %fusion.13 = bf16[512,2048]{1,0:T(8,128)(2,1)} fusion(bf16[512,768]{1,0:T(8,128)(2,1)} %copy-done.3, bf16[1,768,2048]{2,1,0:T(8,128)(2,1)} %param.12), kind=kOutput, calls=%fused_computation.18 | convolution fusion | flops 1611661312 | bytes 6029312 | tf_op jit(solution)/shard_map/dot_general | solution.py:74
  165.0 36.7 %all-to-all-done.3 = bf16[16,32,2048]{2,1,0:T(8,128)(2,1)} async-done(((bf16[16,32,2048]{2,1,0:T(8,128)(2,1)}), bf16[16,32,2048]{2,1,0:T(8,128)(2,1)}, u32[]{:S(2)}, u32[]{:S(2)}) %all-to-all-start.3) | async-done | bytes 2097184 | tf_op jit(solution)/shard_map/all_to_all | solution.py:99
  201.7 5.1 %all-to-all-start.1 = ((bf16[16,32,2048]{2,1,0:T(8,128)(2,1)}), bf16[16,32,2048]{2,1,0:T(8,128)(2,1)}, u32[]{:S(2)}, u32[]{:S(2)}) async-start(bf16[16,32,2048]{2,1,0:T(8,128)(2,1)} %bitcast.73), calls=%async_computation.1 | async-start | bytes 4194304 | tf_op jit(solution)/shard_map/all_to_all | solution.py:78
  206.8 0.3 select_reduce_fusion
  207.2 2.9 %convolution_convert_fusion.5 = bf16[56,2048]{1,0:T(8,128)(2,1)} fusion(pred[512,56]{0,1:T(8,128)(4,1)S(1)} %fusion.24, bf16[512,2048]{1,0:T(8,128)(2,1)} %bitcast.12), kind=kOutput, calls=%fused_computation.24 | convolution fusion | flops 117555200 | bytes 2355200 | tf_op jit(solution)/shard_map/dot_general | solution.py:100
  210.0 44.1 %all-to-all-done.1 = bf16[16,32,2048]{2,1,0:T(8,128)(2,1)} async-done(((bf16[16,32,2048]{2,1,0:T(8,128)(2,1)}), bf16[16,32,2048]{2,1,0:T(8,128)(2,1)}, u32[]{:S(2)}, u32[]{:S(2)}) %all-to-all-start.1) | async-done | bytes 2097184 | tf_op jit(solution)/shard_map/all_to_all | solution.py:78
  254.2 3.5 %convolution_convert_fusion.6 = bf16[56,2048]{1,0:T(8,128)(2,1)} fusion(f32[512,56]{0,1:T(8,128)S(1)} %select_reduce_fusion, bf16[512,2048]{1,0:T(8,128)(2,1)} %bitcast.7), kind=kOutput, calls=%fused_computation.25 | convolution fusion | flops 704757760 | bytes 2441216 | tf_op jit(solution)/shard_map/dot_general | solution.py:79
  257.7 13.4 %reduce-scatter.6.cloned.1.call-done = bf16[1,1024,768]{2,1,0:T(8,128)(2,1)} async-done(((bf16[1,2048,768]{2,1,0:T(8,128)(2,1)}), bf16[1,1024,768]{2,1,0:T(8,128)(2,1)}) %reduce-scatter.6.cloned.1.call-update) | async-done | bytes 1572880 | tf_op jit(solution)/shard_map/reduce_scatter | solution.py:108
  (28 shorter events, 0.6 us)
Async XLA Ops:
  7.2 117.8 %copy-start = (bf16[1,2048,768]{2,1,0:T(8,128)(2,1)S(1)}, bf16[1,2048,768]{2,1,0:T(8,128)(2,1)}, u32[]{:S(2)}) copy-start(bf16[1,2048,768]{2,1,0:T(8,128)(2,1)} %param.10) | copy-start | bytes 9437188
  14.3 6.5 %copy-start.1 = (s32[56,8]{0,1:T(8,128)S(1)}, s32[56,8]{0,1:T(8,128)}, u32[]{:S(2)}) copy-start(s32[56,8]{0,1:T(8,128)} %param.8) | copy-start | bytes 5380
  14.3 53.7 %all-to-all-start.2 = ((bf16[16,32,2048]{2,1,0:T(8,128)(2,1)}), bf16[16,32,2048]{2,1,0:T(8,128)(2,1)}, u32[]{:S(2)}, u32[]{:S(2)}) async-start(bf16[16,32,2048]{2,1,0:T(8,128)(2,1)} %bitcast.72), calls=%async_computation.2 | async-start | bytes 4194304 | tf_op jit(solution)/shard_map/all_to_all | solution.py:86
  68.1 52.4 %all-to-all-start = ((bf16[16,32,2048]{2,1,0:T(8,128)(2,1)}), bf16[16,32,2048]{2,1,0:T(8,128)(2,1)}, u32[]{:S(2)}, u32[]{:S(2)}) async-start(bf16[16,32,2048]{2,1,0:T(8,128)(2,1)} %bitcast.70), calls=%async_computation | async-start | bytes 4194304 | tf_op jit(solution)/shard_map/all_to_all | solution.py:70
  73.1 184.5 %reduce-scatter.8.cloned.1.call-start = ((), (), s32[]{:S(2)}) async-start(), calls=%async_computation.9 | async-start | bytes 4718592 | tf_op jit(solution)/shard_map/reduce_scatter | solution.py:109
  120.5 4.4 %copy-start.4 = (f32[512,768]{1,0:T(8,128)S(1)}, f32[512,768]{1,0:T(8,128)}, u32[]{:S(2)}) copy-start(f32[512,768]{1,0:T(8,128)} %fusion.1) | copy-start | bytes 4718596
  130.0 0.9 copy-start.3
  136.1 121.6 %reduce-scatter.4.cloned.1.call-start = ((), (), s32[]{:S(2)}) async-start(), calls=%async_computation.7 | async-start | bytes 4718592 | tf_op jit(solution)/shard_map/reduce_scatter | solution.py:107
  141.6 4.9 %copy-start.2 = (bf16[512,768]{1,0:T(8,128)(2,1)S(1)}, bf16[512,768]{1,0:T(8,128)(2,1)}, u32[]{:S(2)}) copy-start(bf16[512,768]{1,0:T(8,128)(2,1)} %get-tuple-element.5) | copy-start | bytes 2359300
  149.7 52.0 %all-to-all-start.3 = ((bf16[16,32,2048]{2,1,0:T(8,128)(2,1)}), bf16[16,32,2048]{2,1,0:T(8,128)(2,1)}, u32[]{:S(2)}, u32[]{:S(2)}) async-start(bf16[16,32,2048]{2,1,0:T(8,128)(2,1)} %bitcast.71), calls=%async_computation.3 | async-start | bytes 4194304 | tf_op jit(solution)/shard_map/all_to_all | solution.py:99
  154.4 116.7 %reduce-scatter.6.cloned.1.call-start = ((), (), s32[]{:S(2)}) async-start(), calls=%async_computation.8 | async-start | bytes 4718592 | tf_op jit(solution)/shard_map/reduce_scatter | solution.py:108
  201.7 52.4 %all-to-all-start.1 = ((bf16[16,32,2048]{2,1,0:T(8,128)(2,1)}), bf16[16,32,2048]{2,1,0:T(8,128)(2,1)}, u32[]{:S(2)}, u32[]{:S(2)}) async-start(bf16[16,32,2048]{2,1,0:T(8,128)(2,1)} %bitcast.73), calls=%async_computation.1 | async-start | bytes 4194304 | tf_op jit(solution)/shard_map/all_to_all | solution.py:78
Sparse Core Ops, SparseCore 0:
  136.2 42.3 reduce-scatter.7
  181.5 43.3 reduce-scatter.3
  227.7 43.3 reduce-scatter.5
where the time goes:
time: 281 us; the launch traced here: 278 us
  waiting for transfers between devices  180 us (64%)
  matrix products  56.2 us (20%)
  starting transfers between devices  21.4 us (8%)
  between operations  13.9 us (5%)
  local copies, waits for them, and re-layouts  3.25 us (1%)
  other arithmetic  2.99 us (1%)
    all_to_all x1, waiting for transfers between devices, on_device(): lax.all_to_all(out_slots, 'expert', split_axis=0, concat_axis=0, tiled=True)  44.1 us
    all_to_all x1, waiting for transfers between devices, on_device(): lax.all_to_all(jnp.dot(assign_table, cot_rows, preferred_element_type=jnp...  43.7 us
    all_to_all x1, waiting for transfers between devices, on_device(): lax.all_to_all(x_slots, 'expert', split_axis=0, concat_axis=0, tiled=True)  41.8 us
    all_to_all x1, waiting for transfers between devices, on_device(): lax.all_to_all(d_slots, 'expert', split_axis=0, concat_axis=0, tiled=True)  36.7 us
    reduce_scatter x1, waiting for transfers between devices, on_device(): lax.psum_scatter(grad_u[None], 'dp', scatter_dimension=1, tiled=True)  13.4 us
    all_to_all x1, starting transfers between devices, on_device(): lax.all_to_all(jnp.dot(assign_table, cot_rows, preferred_element_type=jnp...  6.37 us
  transfers between devices with their start and end apart: 7, of which 5 were waited for; matrix products, arithmetic and copies ran while one was open for 14% of the time, Pallas kernels for 0%

commit v1 on v0

v1 whole, which is shorter than its diff:
```python
import functools

import jax
import jax.numpy as jnp
from jax import lax
from jax.sharding import PartitionSpec as P

def dot_nn(a, b):
    return jnp.dot(a, b, preferred_element_type=jnp.float32)


def dot_nt(a, b):
    return lax.dot_general(a, b, (((1,), (1,)), ((), ())), preferred_element_type=jnp.float32)


def dot_tn(a, b):
    return lax.dot_general(a, b, (((0,), (0,)), ((), ())), preferred_element_type=jnp.float32)


def weight_table(expert_ids, combine, n_experts):
    named = expert_ids[:, :, None] == jnp.arange(n_experts, dtype=jnp.int32)
    return jnp.sum(jnp.where(named, combine[:, :, None], 0.0), axis=1)


def on_device(wide, tokens, expert_ids, combine, w_gate, w_up, w_down, grad_out):
    n_experts = lax.axis_size("expert")
    d = lax.axis_index("dp")
    e = lax.axis_index("expert")
    width = tokens.shape[1]
    half = width // lax.axis_size("dp")
    own_rows = tokens.shape[0] * n_experts
    wg, wu, wd = w_gate[0], w_up[0], w_down[0]
    axes = ("dp", "expert") if wide else "expert"

    table_all = lax.all_gather(weight_table(expert_ids, combine, n_experts), axes, axis=0, tiled=True)
    x_all = lax.all_gather(tokens, axes, axis=0, tiled=True)
    g_all = lax.all_gather(grad_out, axes, axis=0, tiled=True)
    weight = lax.dynamic_slice_in_dim(table_all, e, 1, axis=1)

    def own(a):
        return lax.dynamic_slice_in_dim(a, d * own_rows, own_rows, axis=0) if wide else a

    def my_half(a):
        return lax.dynamic_slice_in_dim(a, d * half, half, axis=1) if wide else a

    gate = dot_nn(x_all, wg)
    upper = dot_nn(x_all, wu)
    sigma = jax.nn.sigmoid(gate)
    hidden = (gate * sigma * upper).astype(jnp.bfloat16)
    part = (own(weight) * dot_nn(own(hidden), wd)).astype(jnp.bfloat16)
    mixed = lax.psum_scatter(part, "expert", scatter_dimension=0, tiled=True)

    cotangent = (weight * g_all.astype(jnp.float32)).astype(jnp.bfloat16)
    d_hidden = dot_nt(cotangent, wd)
    d_gate = (d_hidden * upper * sigma * (1.0 + gate * (1.0 - sigma))).astype(jnp.bfloat16)
    d_upper = (d_hidden * gate * sigma).astype(jnp.bfloat16)
    d_rows = (dot_nt(own(d_gate), wg) + dot_nt(own(d_upper), wu)).astype(jnp.bfloat16)
    grad_tokens = lax.psum_scatter(d_rows, "expert", scatter_dimension=0, tiled=True)
    x_half = my_half(x_all)
    grad_g = dot_tn(x_half, d_gate).astype(jnp.bfloat16)
    grad_u = dot_tn(x_half, d_upper).astype(jnp.bfloat16)
    grad_d = dot_tn(hidden, my_half(cotangent)).astype(jnp.bfloat16)
    if not wide:
        grad_g = lax.psum_scatter(grad_g, "dp", scatter_dimension=0, tiled=True)
        grad_u = lax.psum_scatter(grad_u, "dp", scatter_dimension=0, tiled=True)
        grad_d = lax.psum_scatter(grad_d, "dp", scatter_dimension=1, tiled=True)
    return mixed, grad_tokens, grad_g[None], grad_u[None], grad_d[None]


def solution(mesh):
    rows = P(("dp", "expert"), None)
    expert = P("expert", None, None)
    return jax.shard_map(
        functools.partial(on_device, mesh.shape["dp"] == 2),
        mesh=mesh,
        in_specs=(rows, rows, rows, expert, expert, expert, rows),
        out_specs=(rows, rows, P("expert", "dp", None), P("expert", "dp", None), P("expert", None, "dp")),
        check_vma=False,
    )
```

time: 281 us -> 334 us (1.19)
  blocking collectives: 0 us -> 34.1 us
  waiting for transfers between devices: 180 us -> 208 us
  starting transfers between devices: 21.4 us -> 0.34 us
  matrix products: 56.2 us -> 68 us
    all_to_all x4 -> x0, waiting for transfers between devices: 166 us -> none  [the longest x1 44.1 us: on_device(): lax.all_to_all(out_slots, 'expert', split_axis=0, concat_axis=0, tiled=True)]
    all_gather x0 -> x2, waiting for transfers between devices: none -> 97.5 us  [the longest x1 56.7 us: on_device(): g_all = lax.all_gather(grad_out, axes, axis=0, tiled=True)]
    reduce_scatter x3 -> x2, waiting for transfers between devices: 13.4 us -> 109 us  [the longest x1 72.4 us: on_device(): lax.psum_scatter(d_rows, 'expert', scatter_dimension=0, tiled=True)]
    all_gather x0 -> x1, blocking collectives: none -> 34.1 us  [on_device(): lax.all_gather(weight_table(expert_ids, combine, n_experts), axes, axis=0...]
    all_to_all x4 -> x0, starting transfers between devices: 21.1 us -> none  [the longest x1 6.37 us: on_device(): lax.all_to_all(jnp.dot(assign_table, cot_rows, preferred_element_type=jnp...]
    dot_general x13 -> x9, matrix products: 56.2 us -> 68 us  [the longest x3 24.8 us: dot_nt(): lax.dot_general(a, b, (((1,), (1,)), ((), ())), preferred_element_type=jn...]
    convert_element_type x1, other arithmetic: 0.97 us -> 4.33 us  [on_device(): cotangent = (weight * g_all.astype(jnp.float32)).astype(jnp.bfloat16)]
  transfers between devices with their start and end apart: 7 -> 4, of which waited for: 5 -> 4; matrix products, arithmetic and copies ran while one was open for 14% -> 15% of each run, Pallas kernels for 0% -> 0%
where the time goes in v1:
time: 334 us; the launch traced here: 331 us
  waiting for transfers between devices  208 us (62%)
  matrix products  68 us (20%)
  blocking collectives  34.1 us (10%)
  between operations  13.9 us (4%)
  other arithmetic  5.05 us (2%)
    reduce_scatter x1, waiting for transfers between devices, on_device(): lax.psum_scatter(d_rows, 'expert', scatter_dimension=0, tiled=True)  72.4 us
    all_gather x1, waiting for transfers between devices, on_device(): g_all = lax.all_gather(grad_out, axes, axis=0, tiled=True)  56.7 us
    all_gather x1, waiting for transfers between devices, on_device(): x_all = lax.all_gather(tokens, axes, axis=0, tiled=True)  40.8 us
    reduce_scatter x1, waiting for transfers between devices, on_device(): mixed = lax.psum_scatter(part, 'expert', scatter_dimension=0, tiled=True)  36.8 us
    all_gather x1, blocking collectives, on_device(): lax.all_gather(weight_table(expert_ids, combine, n_experts), axes, axis=0...  34.1 us
    dot_general x3, matrix products, dot_nt(): lax.dot_general(a, b, (((1,), (1,)), ((), ())), preferred_element_type=jn...  24.8 us
    dot_general x3, matrix products, dot_nn(): return jnp.dot(a, b, preferred_element_type=jnp.float32)  22.8 us
    dot_general x3, matrix products, dot_tn(): lax.dot_general(a, b, (((0,), (0,)), ((), ())), preferred_element_type=jn...  20.4 us
  transfers between devices with their start and end apart: 4, of which 4 were waited for; matrix products, arithmetic and copies ran while one was open for 15% of the time, Pallas kernels for 0%

profile of v1, /device:TPU:14, one launch (start us, length us, event | category | flops | bytes accessed | tf_op | source)
XLA Modules:
  0.0 331.3 jit_solution(17125149857260408760)
XLA Ops:
  7.2 0.0 copy-start
  7.2 0.0 all-gather.4.cloned.1.call-start
  7.2 0.7 all-gather.4.cloned.1.call-update
  7.9 0.0 all-gather.6.cloned.1.call-start
  8.0 0.7 all-gather.6.cloned.1.call-update
  8.7 0.0 reduce-scatter.3.cloned.1.call-start
  8.7 0.7 select_reduce_fusion
  9.4 34.1 %all-gather = f32[32,56,16]{1,2,0:T(8,128)S(1)} all-gather(f32[1,56,16]{1,2,0:T(8,128)S(1)} %bitcast.32), channel_id=1, replica_groups=mesh['dp'=2,'expert'=16] {'dp','expert'}, dimensions={0}, use_global_device_ids=true | all-gather | bytes 118272 | tf_op jit(solution)/shard_map/all_gather | solution.py:35
  43.5 0.1 copy.21
  43.6 0.2 reshape.13
  43.8 0.1 dynamic-slice_reduce_fusion.1
  43.9 40.8 %all-gather.4.cloned.1.call-done = bf16[1792,2048]{1,0:T(8,128)(2,1)} async-done(((bf16[56,2048]{1,0:T(8,128)(2,1)}), bf16[1792,2048]{1,0:T(8,128)(2,1)}) %all-gather.4.cloned.1.call-update) | async-done | bytes 7340048 | tf_op jit(solution)/shard_map/all_gather | solution.py:36
  84.7 10.8 %fusion.10 = f32[1792,768]{1,0:T(8,128)} fusion(bf16[1792,2048]{1,0:T(8,128)(2,1)} %all-gather.4.cloned.1.call-done, bf16[1,2048,768]{2,1,0:T(8,128)(2,1)} %param.11), kind=kOutput, calls=%fused_computation.17 | convolution fusion | flops 5637144576 | bytes 15990784 | tf_op jit(solution)/shard_map/dot_general | solution.py:9
  95.5 0.0 copy-done.3
  95.5 7.5 %fusion.14 = f32[1792,768]{1,0:T(8,128)} fusion(bf16[1792,2048]{1,0:T(8,128)(2,1)S(1)} %copy-done.2, bf16[1,2048,768]{2,1,0:T(8,128)(2,1)S(1)} %copy-done.3), kind=kOutput, calls=%fused_computation.21 | convolution fusion | flops 5637144576 | bytes 15990784 | tf_op jit(solution)/shard_map/dot_general | solution.py:9
  103.1 56.7 %all-gather.6.cloned.1.call-done = bf16[1792,2048]{1,0:T(8,128)(2,1)} async-done(((bf16[56,2048]{1,0:T(8,128)(2,1)}), bf16[1792,2048]{1,0:T(8,128)(2,1)}) %all-gather.6.cloned.1.call-update) | async-done | bytes 7340048 | tf_op jit(solution)/shard_map/all_gather | solution.py:37
  159.7 4.3 %multiply_convert_fusion = bf16[1792,2048]{1,0:T(8,128)(2,1)S(1)} fusion(bf16[1792,2048]{1,0:T(8,128)(2,1)} %all-gather.6.cloned.1.call-done, f32[1792]{0:T(1024)S(1)} %dynamic-slice_reduce_fusion), kind=kLoop, calls=%fused_computation | loop fusion | flops 11010048 | bytes 14687232 | tf_op jit(solution)/shard_map/convert_element_type | solution.py:53
  164.1 0.0 copy-done
  164.1 14.7 %multiply_convert_fusion.2 = (bf16[1792,768]{1,0:T(8,128)(2,1)}, bf16[1792,768]{1,0:T(8,128)(2,1)}, bf16[1792,768]{1,0:T(8,128)(2,1)S(1)}) fusion(f32[1792,768]{1,0:T(8,128)} %fusion.14, f32[1792,768]{1,0:T(8,128)} %fusion.10, bf16[1792,2048]{1,0:T(8,128)(2,1)S(1)} %multiply_convert_fusion, bf16[1,768,2048]{2,1,0:T(8,128)(2,1)S(1)} %copy-done), kind=kOutput, calls=%fused_computation.3 | convolution fusion | flops 5659164672 | bytes 29753344 | tf_op jit(solution)/shard_map/dot_general | solution.py:13
  178.8 1.5 copy-done.8
  180.3 4.5 %multiply_convert_fusion.1 = bf16[896,2048]{1,0:T(8,128)(2,1)} fusion(f32[896]{0:T(1024)S(1)} %dynamic-slice_reduce_fusion.1, bf16[1,768,2048]{2,1,0:T(8,128)(2,1)S(1)} %copy-done, bf16[1792,768]{1,0:T(8,128)(2,1)S(1)} %get-tuple-element.7, s32[]{:T(128)S(6)} %select_n.22), kind=kOutput, calls=%fused_computation.2 | convolution fusion | flops 2822242304 | bytes 8196100 | tf_op jit(solution)/shard_map/dot_general | solution.py:9
  184.8 0.0 reduce-scatter.3.cloned.1.call-update
  184.8 0.2 reduce-scatter.5.cloned.1.call-start
  185.0 0.0 copy-start.4
  185.0 5.5 %fusion.12 = f32[896,2048]{1,0:T(8,128)S(1)} fusion(bf16[1,2048,768]{2,1,0:T(8,128)(2,1)} %param.10, bf16[1792,768]{1,0:T(8,128)(2,1)} %get-tuple-element.6, s32[]{:T(128)S(6)} %select_n.22), kind=kOutput, calls=%fused_computation.19 | convolution fusion | flops 2818572288 | bytes 11862020 | tf_op jit(solution)/shard_map/dot_general | solution.py:13
  190.6 4.6 %add_convert_fusion = bf16[896,2048]{1,0:T(8,128)(2,1)} fusion(f32[896,2048]{1,0:T(8,128)S(1)} %fusion.12, bf16[1,2048,768]{2,1,0:T(8,128)(2,1)S(1)} %copy-done.4, bf16[1792,768]{1,0:T(8,128)(2,1)S(1)} %copy-done.6, s32[]{:T(128)S(6)} %select_n.22), kind=kOutput, calls=%fused_computation.1 | convolution fusion | flops 2822242304 | bytes 15532036 | tf_op jit(solution)/shard_map/dot_general | solution.py:13
  195.2 0.0 reduce-scatter.5.cloned.1.call-update
  195.2 7.5 %fusion.25 = bf16[1,768,1024]{2,1,0:T(8,128)(2,1)} fusion(bf16[1792,768]{1,0:T(8,128)(2,1)} %copy-done.8, bf16[1792,2048]{1,0:T(8,128)(2,1)} %copy-done.1, s32[]{:T(128)S(6)} %select_n.26), kind=kOutput, calls=%fused_computation.26 | convolution fusion | flops 2819358720 | bytes 7995396 | tf_op jit(solution)/shard_map/dot_general | solution.py:17
  202.7 6.6 %fusion.28 = bf16[1,1024,768]{2,1,0:T(8,128)(2,1)} fusion(bf16[1792,768]{1,0:T(8,128)(2,1)S(1)} %copy-done.7, bf16[1792,2048]{1,0:T(8,128)(2,1)} %all-gather.4.cloned.1.call-done, s32[]{:T(128)S(6)} %select_n.26), kind=kOutput, calls=%fused_computation.27 | convolution fusion | flops 2819358720 | bytes 7995396 | tf_op jit(solution)/shard_map/dot_general | solution.py:17
  209.3 6.3 %fusion.31 = bf16[1,1024,768]{2,1,0:T(8,128)(2,1)} fusion(bf16[1792,768]{1,0:T(8,128)(2,1)S(1)} %copy-done.5, bf16[1792,2048]{1,0:T(8,128)(2,1)} %all-gather.4.cloned.1.call-done, s32[]{:T(128)S(6)} %select_n.26), kind=kOutput, calls=%fused_computation.28 | convolution fusion | flops 2819358720 | bytes 7995396 | tf_op jit(solution)/shard_map/dot_general | solution.py:17
  215.6 36.8 %reduce-scatter.3.cloned.1.call-done = bf16[56,2048]{1,0:T(8,128)(2,1)} async-done(((bf16[896,2048]{1,0:T(8,128)(2,1)}), bf16[56,2048]{1,0:T(8,128)(2,1)}) %reduce-scatter.3.cloned.1.call-update) | async-done | bytes 229392 | tf_op jit(solution)/shard_map/reduce_scatter | solution.py:51
  252.4 72.4 %reduce-scatter.5.cloned.1.call-done = bf16[56,2048]{1,0:T(8,128)(2,1)} async-done(((bf16[896,2048]{1,0:T(8,128)(2,1)}), bf16[56,2048]{1,0:T(8,128)(2,1)}) %reduce-scatter.5.cloned.1.call-update) | async-done | bytes 229392 | tf_op jit(solution)/shard_map/reduce_scatter | solution.py:58
  (14 shorter events, 0.1 us)
Async XLA Ops:
  7.2 156.9 %copy-start = (bf16[1,768,2048]{2,1,0:T(8,128)(2,1)S(1)}, bf16[1,768,2048]{2,1,0:T(8,128)(2,1)}, u32[]{:S(2)}) copy-start(bf16[1,768,2048]{2,1,0:T(8,128)(2,1)} %param.12) | copy-start | bytes 9437188
  7.2 77.6 %all-gather.4.cloned.1.call-start = ((), (), s32[]{:S(2)}) async-start(), calls=%async_computation.2 | async-start | bytes 7569408 | tf_op jit(solution)/shard_map/all_gather | solution.py:36
  7.9 151.8 %all-gather.6.cloned.1.call-start = ((), (), s32[]{:S(2)}) async-start(), calls=%async_computation.4 | async-start | bytes 7569408 | tf_op jit(solution)/shard_map/all_gather | solution.py:37
  8.7 243.7 %reduce-scatter.3.cloned.1.call-start = ((), (), s32[]{:S(2)}) async-start(), calls=%async_computation.3 | async-start | bytes 3899392 | tf_op jit(solution)/shard_map/reduce_scatter | solution.py:51
  84.7 10.8 %copy-start.2 = (bf16[1792,2048]{1,0:T(8,128)(2,1)S(1)}, bf16[1792,2048]{1,0:T(8,128)(2,1)}, u32[]{:S(2)}) copy-start(bf16[1792,2048]{1,0:T(8,128)(2,1)} %all-gather.4.cloned.1.call-done) | copy-start | bytes 22020100
  84.7 10.8 %copy-start.3 = (bf16[1,2048,768]{2,1,0:T(8,128)(2,1)S(1)}, bf16[1,2048,768]{2,1,0:T(8,128)(2,1)}, u32[]{:S(2)}) copy-start(bf16[1,2048,768]{2,1,0:T(8,128)(2,1)} %param.10) | copy-start | bytes 9437188
  164.1 14.7 %copy-start.1 = (bf16[1792,2048]{1,0:T(8,128)(2,1)}, bf16[1792,2048]{1,0:T(8,128)(2,1)S(1)}, u32[]{:S(2)}) copy-start(bf16[1792,2048]{1,0:T(8,128)(2,1)S(1)} %multiply_convert_fusion) | copy-start | bytes 22020100
  178.8 1.5 copy-start.8
  184.8 140.0 %reduce-scatter.5.cloned.1.call-start = ((), (), s32[]{:S(2)}) async-start(), calls=%async_computation.5 | async-start | bytes 3899392 | tf_op jit(solution)/shard_map/reduce_scatter | solution.py:58
  185.0 5.5 %copy-start.4 = (bf16[1,2048,768]{2,1,0:T(8,128)(2,1)S(1)}, bf16[1,2048,768]{2,1,0:T(8,128)(2,1)}, u32[]{:S(2)}) copy-start(bf16[1,2048,768]{2,1,0:T(8,128)(2,1)} %param.11) | copy-start | bytes 9437188
  185.0 5.5 %copy-start.6 = (bf16[1792,768]{1,0:T(8,128)(2,1)S(1)}, bf16[1792,768]{1,0:T(8,128)(2,1)}, u32[]{:S(2)}) copy-start(bf16[1792,768]{1,0:T(8,128)(2,1)} %get-tuple-element.5) | copy-start | bytes 8257540
  195.2 7.5 %copy-start.7 = (bf16[1792,768]{1,0:T(8,128)(2,1)S(1)}, bf16[1792,768]{1,0:T(8,128)(2,1)}, u32[]{:S(2)}) copy-start(bf16[1792,768]{1,0:T(8,128)(2,1)} %get-tuple-element.5) | copy-start | bytes 8257540
  202.7 6.6 %copy-start.5 = (bf16[1792,768]{1,0:T(8,128)(2,1)S(1)}, bf16[1792,768]{1,0:T(8,128)(2,1)}, u32[]{:S(2)}) copy-start(bf16[1792,768]{1,0:T(8,128)(2,1)} %get-tuple-element.6) | copy-start | bytes 8257540
Sparse Core Ops, SparseCore 0:
  10.9 73.7 all-gather.3
  87.6 72.0 all-gather.5
  184.9 67.4 reduce-scatter.2
  257.1 67.5 reduce-scatter.4

commit v2 on v1

v2 whole, which is shorter than its diff:
```python
import jax
import jax.numpy as jnp
from jax import lax
from jax.experimental import pallas as pl
from jax.experimental.pallas import tpu as pltpu
from jax.sharding import PartitionSpec as P

def dot_nn(a, b):
    return jnp.dot(a, b, preferred_element_type=jnp.float32)


def dot_nt(a, b):
    return lax.dot_general(a, b, (((1,), (1,)), ((), ())), preferred_element_type=jnp.float32)


def dot_tn(a, b):
    return lax.dot_general(a, b, (((0,), (0,)), ((), ())), preferred_element_type=jnp.float32)


def weight_table(expert_ids, combine, n_experts):
    named = expert_ids[:, :, None] == jnp.arange(n_experts, dtype=jnp.int32)
    return jnp.sum(jnp.where(named, combine[:, :, None], 0.0), axis=1)


def on_device(tokens, expert_ids, combine, w_gate, w_up, w_down, grad_out):
    n_experts = lax.axis_size("expert")
    e = lax.axis_index("expert")
    wg, wu, wd = w_gate[0], w_up[0], w_down[0]

    table_all = lax.all_gather(weight_table(expert_ids, combine, n_experts), "expert", axis=0, tiled=True)
    x_all = lax.all_gather(tokens, "expert", axis=0, tiled=True)
    g_all = lax.all_gather(grad_out, "expert", axis=0, tiled=True)
    weight = lax.dynamic_slice_in_dim(table_all, e, 1, axis=1)

    gate = dot_nn(x_all, wg)
    upper = dot_nn(x_all, wu)
    sigma = jax.nn.sigmoid(gate)
    hidden = (gate * sigma * upper).astype(jnp.bfloat16)
    part = (weight * dot_nn(hidden, wd)).astype(jnp.bfloat16)
    mixed = lax.psum_scatter(part, "expert", scatter_dimension=0, tiled=True)

    cotangent = (weight * g_all.astype(jnp.float32)).astype(jnp.bfloat16)
    d_hidden = dot_nt(cotangent, wd)
    d_gate = (d_hidden * upper * sigma * (1.0 + gate * (1.0 - sigma))).astype(jnp.bfloat16)
    d_upper = (d_hidden * gate * sigma).astype(jnp.bfloat16)
    d_rows = (dot_nt(d_gate, wg) + dot_nt(d_upper, wu)).astype(jnp.bfloat16)
    grad_tokens = lax.psum_scatter(d_rows, "expert", scatter_dimension=0, tiled=True)
    grad_g = dot_tn(x_all, d_gate).astype(jnp.bfloat16)
    grad_u = dot_tn(x_all, d_upper).astype(jnp.bfloat16)
    grad_d = dot_tn(hidden, cotangent).astype(jnp.bfloat16)
    grad_g = lax.psum_scatter(grad_g, "dp", scatter_dimension=0, tiled=True)
    grad_u = lax.psum_scatter(grad_u, "dp", scatter_dimension=0, tiled=True)
    grad_d = lax.psum_scatter(grad_d, "dp", scatter_dimension=1, tiled=True)
    return mixed, grad_tokens, grad_g[None], grad_u[None], grad_d[None]


ROWS = 64
TILE = 256
Z, XD, YD, SD = 0, 3, 7, 15
LANES = 128


def fused_kernel(x_in, g_in, wg_hbm, wu_hbm, wd_hbm, mixed_out, gt_out, gg_out, gu_out, gd_out,
                 xs, gs, wg, wu, wd, hid, dg, du, part, s1, s2, s3,
                 wsem, send, recv, rsend, rrecv):
    width = g_in.shape[1]
    half = width // 2
    d = lax.axis_index("dp")
    e = lax.axis_index("expert")
    z, y, c = e // 4, (e // 2) % 2, e % 2

    def peer(rx, ry, rz, rc):
        return ((d + rx) % 2, (((z + rz) % 4) * 2 + (y + ry) % 2) * 2 + (c + rc) % 2)

    sibling, across_y, across_x = peer(0, 0, 0, 1), peer(0, 1, 0, 0), peer(1, 0, 0, 0)
    partners = [peer(0, 0, rz, 0) for rz in (1, 2, 3)] + [sibling, across_y, across_x]

    loads = [pltpu.make_async_copy(src, dst, wsem.at[i])
             for i, (src, dst) in enumerate(((wg_hbm, wg), (wu_hbm, wu), (wd_hbm, wd)))]
    for load in loads:
        load.start()
    barrier = pltpu.get_barrier_semaphore()
    for partner in partners:
        pl.semaphore_signal(barrier, inc=1, device_id=partner, device_id_type=pl.DeviceIdType.MESH)
    xs[0, 0:ROWS, :] = x_in[...]
    gs[0, 0:ROWS, :] = g_in[...]
    pl.semaphore_wait(barrier, len(partners))

    slots = (xs, gs)

    def shard(a, tile, rz):
        return slots[a].at[tile, pl.ds(rz * ROWS, ROWS)]

    def copy(a, src, dst, sem, device):
        return pltpu.make_async_remote_copy(
            src_ref=shard(a, *src), dst_ref=shard(a, *dst), send_sem=send.at[a, sem],
            recv_sem=recv.at[a, sem], device_id=device, device_id_type=pl.DeviceIdType.MESH)

    def along_z(a, rz):
        return copy(a, (0, 0), (0, 4 - rz), Z + 3 - rz, peer(0, 0, rz, 0))

    def along_y(a, rz):
        return copy(a, (0, rz), (2, rz), XD + rz, across_y)

    def along_x(a, ry, rz):
        return copy(a, (2 * ry, rz), (4 + 2 * ry, rz), YD + 4 * ry + rz, across_x)

    def to_core(a, rx, ry, rz):
        return copy(a, (4 * rx + 2 * ry, rz), (4 * rx + 2 * ry + 1, rz), SD + 8 * rx + 4 * ry + rz, sibling)

    for a in (0, 1):
        for rz in (2, 1, 3):
            along_z(a, rz).start()
        along_y(a, 0).start()
        along_x(a, 0, 0).start()
        to_core(a, 0, 0, 0).start()
    for a in (0, 1):
        for rz in (1, 3, 2):
            along_z(a, 4 - rz).wait_recv()
            along_y(a, rz).start()
            along_x(a, 0, rz).start()
            to_core(a, 0, 0, rz).start()
    for a in (0, 1):
        for rz in (0, 1, 3, 2):
            along_y(a, rz).wait_recv()
            along_x(a, 1, rz).start()
            to_core(a, 0, 1, rz).start()
    for load in loads:
        load.wait()

    lane = lax.broadcasted_iota(jnp.int32, (TILE, LANES), 1)
    mine = (lane < 48) & (lane % 16 == e)

    def tile_pass(tile, own):
        x = xs[tile, :, 0:width]
        side = xs[tile, :, width:width + LANES].astype(jnp.float32)
        weight = jnp.sum(jnp.where(mine, side, 0.0), axis=1, keepdims=True)
        gate = dot_nn(x, wg[...])
        upper = dot_nn(x, wu[...])
        sigma = jax.nn.sigmoid(gate)
        silu = gate * sigma
        hidden = (silu * upper * weight).astype(jnp.bfloat16)
        hid[tile] = hidden
        d_hidden = weight * dot_nt(gs[tile], wd[...])
        d_gate = (d_hidden * upper * sigma * (1.0 + gate * (1.0 - sigma))).astype(jnp.bfloat16)
        d_upper = (d_hidden * silu).astype(jnp.bfloat16)
        dg[tile] = d_gate
        du[tile] = d_upper
        if own:
            part[0, tile] = dot_nn(hidden, wd[...]).astype(jnp.bfloat16)
            part[1, tile] = (dot_nt(d_gate, wg[...]) + dot_nt(d_upper, wu[...])).astype(jnp.bfloat16)

    def chunk(rx, ry):
        for a in (0, 1):
            for rz in range(4):
                to_core(a, rx, ry, rz).wait_recv()
        first = 4 * rx + 2 * ry

        def step(i, carry):
            tile_pass(first + i, rx == 0)
            return carry

        lax.fori_loop(0, 2, step, 0)

    def rcopy(src, dst, a, sem, device):
        return pltpu.make_async_remote_copy(
            src_ref=src, dst_ref=dst, send_sem=rsend.at[a, sem], recv_sem=rrecv.at[a, sem],
            device_id=device, device_id_type=pl.DeviceIdType.MESH)

    def sum_core(a, ry):
        return rcopy(part.at[a, 2 * ry + 1], s1.at[a, ry], a, ry, sibling)

    def sum_y(a):
        return rcopy(part.at[a, 2], s2.at[a], a, 2, across_y)

    def sum_z(a, rz):
        return rcopy(part.at[a, 0, pl.ds(rz * ROWS, ROWS)], s3.at[a, 3 - rz], a, 2 + rz, peer(0, 0, rz, 0))

    def add(a, tile, other):
        total = part[a, tile].astype(jnp.float32) + other.astype(jnp.float32)
        part[a, tile] = total.astype(jnp.bfloat16)

    def from_x(ry):
        for a in (0, 1):
            for rz in (0, 1, 3, 2):
                along_x(a, ry, rz).wait_recv()
                to_core(a, 1, ry, rz).start()

    chunk(0, 0)
    for a in (0, 1):
        sum_core(a, 0).start()
    chunk(0, 1)
    for a in (0, 1):
        sum_core(a, 1).start()
    from_x(0)
    for a in (0, 1):
        sum_core(a, 1).wait_recv()
        add(a, 2, s1[a, 1])
        sum_y(a).start()
        sum_core(a, 0).wait_recv()
        add(a, 0, s1[a, 0])
    chunk(1, 0)
    for a in (0, 1):
        sum_y(a).wait_recv()
        add(a, 0, s2[a])
        for rz in (1, 2, 3):
            sum_z(a, rz).start()
    from_x(1)
    chunk(1, 1)

    def grads_in(j, carry):
        columns = pl.ds(pl.multiple_of(d * half + j * TILE, TILE), TILE)
        xt = xs[:, :, columns].reshape(8 * TILE, TILE).T
        rows = pl.ds(pl.multiple_of(j * TILE, TILE), TILE)
        gg_out[rows, :] = dot_nn(xt, dg[...].reshape(8 * TILE, -1)).astype(jnp.bfloat16)
        gu_out[rows, :] = dot_nn(xt, du[...].reshape(8 * TILE, -1)).astype(jnp.bfloat16)
        return carry

    lax.fori_loop(0, half // TILE, grads_in, 0)

    def grads_down(j, carry):
        columns = pl.ds(pl.multiple_of(j * TILE, TILE), TILE)
        ht = hid[:, :, columns].reshape(8 * TILE, TILE).T
        mine_half = pl.ds(pl.multiple_of(d * half, half), half)
        gd_out[columns, :] = dot_nn(ht, gs[:, :, mine_half].reshape(8 * TILE, half)).astype(jnp.bfloat16)
        return carry

    lax.fori_loop(0, hid.shape[2] // TILE, grads_down, 0)

    for a, out in ((0, mixed_out), (1, gt_out)):
        total = part[a, 0, 0:ROWS].astype(jnp.float32)
        for rz in (1, 2, 3):
            sum_z(a, rz).wait_recv()
        for i in range(3):
            total = total + s3[a, i].astype(jnp.float32)
        out[...] = total.astype(jnp.bfloat16)

    for a in (0, 1):
        for rz in (1, 2, 3):
            along_z(a, rz).wait_send()
            sum_z(a, rz).wait_send()
        for rz in range(4):
            along_y(a, rz).wait_send()
            for r in (0, 1):
                along_x(a, r, rz).wait_send()
                for rx in (0, 1):
                    to_core(a, rx, r, rz).wait_send()
        for r in (0, 1):
            sum_core(a, r).wait_send()
        sum_y(a).wait_send()


def fused_device(tokens, expert_ids, combine, w_gate, w_up, w_down, grad_out):
    tok, width = tokens.shape
    hidden = w_gate.shape[2]
    table = weight_table(expert_ids, combine, lax.axis_size("expert"))
    high = lax.reduce_precision(table, 8, 7)
    mid = lax.reduce_precision(table - high, 8, 7)
    side = jnp.concatenate([high, mid, table - high - mid], axis=1).astype(jnp.bfloat16)
    x = jnp.pad(jnp.concatenate([tokens, side], axis=1), ((0, ROWS - tok), (0, LANES - side.shape[1])))
    g = jnp.pad(grad_out, ((0, ROWS - tok), (0, 0)))
    bf16 = jnp.bfloat16
    vmem = pl.BlockSpec(memory_space=pltpu.VMEM)
    hbm = pl.BlockSpec(memory_space=pl.ANY)
    mixed, grad_tokens, grad_g, grad_u, grad_d = pl.pallas_call(
        fused_kernel,
        out_shape=[
            jax.ShapeDtypeStruct((ROWS, width), bf16),
            jax.ShapeDtypeStruct((ROWS, width), bf16),
            jax.ShapeDtypeStruct((width // 2, hidden), bf16),
            jax.ShapeDtypeStruct((width // 2, hidden), bf16),
            jax.ShapeDtypeStruct((hidden, width // 2), bf16),
        ],
        in_specs=[vmem, vmem, hbm, hbm, hbm],
        out_specs=[vmem] * 5,
        scratch_shapes=[
            pltpu.VMEM((8, TILE, width + LANES), bf16),
            pltpu.VMEM((8, TILE, width), bf16),
            pltpu.VMEM((width, hidden), bf16),
            pltpu.VMEM((width, hidden), bf16),
            pltpu.VMEM((hidden, width), bf16),
            pltpu.VMEM((8, TILE, hidden), bf16),
            pltpu.VMEM((8, TILE, hidden), bf16),
            pltpu.VMEM((8, TILE, hidden), bf16),
            pltpu.VMEM((2, 4, TILE, width), bf16),
            pltpu.VMEM((2, 2, TILE, width), bf16),
            pltpu.VMEM((2, TILE, width), bf16),
            pltpu.VMEM((2, 3, ROWS, width), bf16),
            pltpu.SemaphoreType.DMA((3,)),
            pltpu.SemaphoreType.DMA((2, 31)),
            pltpu.SemaphoreType.DMA((2, 31)),
            pltpu.SemaphoreType.DMA((2, 6)),
            pltpu.SemaphoreType.DMA((2, 6)),
        ],
        compiler_params=pltpu.CompilerParams(
            collective_id=0, has_side_effects=True, vmem_limit_bytes=63 * 1024 * 1024),
    )(x, g, w_gate[0], w_up[0], w_down[0])
    return mixed[:tok], grad_tokens[:tok], grad_g[None], grad_u[None], grad_d[None]


def solution(mesh):
    rows = P(("dp", "expert"), None)
    expert = P("expert", None, None)
    small = mesh.shape["dp"] == 2 and mesh.shape["expert"] == 16
    return jax.shard_map(
        fused_device if small else on_device,
        mesh=mesh,
        in_specs=(rows, rows, rows, expert, expert, expert, rows),
        out_specs=(rows, rows, P("expert", "dp", None), P("expert", "dp", None), P("expert", None, "dp")),
        check_vma=False,
    )
```

time: 334 us -> 184 us (0.55)
  waiting for transfers between devices: 208 us -> 0 us
  Pallas kernels: 0 us -> 170 us
  matrix products: 68 us -> 0 us
  blocking collectives: 34.1 us -> 0 us
  between operations: 13.9 us -> 0.66 us
  local copies, waits for them, and re-layouts: 1.92 us -> 12.8 us
  other arithmetic: 5.05 us -> 0.74 us
    pallas_call x0 -> x1, Pallas kernels: none -> 170 us  [fused_device(): pl.pallas_call(fused_kernel, out_shape=[jax.ShapeDtypeStruct((ROWS, width...]
    reduce_scatter x2 -> x0, waiting for transfers between devices: 109 us -> none  [the longest x1 72.4 us: on_device(): lax.psum_scatter(d_rows, 'expert', scatter_dimension=0, tiled=True)]
    all_gather x2 -> x0, waiting for transfers between devices: 97.5 us -> none  [the longest x1 56.7 us: on_device(): g_all = lax.all_gather(grad_out, axes, axis=0, tiled=True)]
    dot_general x9 -> x0, matrix products: 68 us -> none  [the longest x3 24.8 us: dot_nt(): lax.dot_general(a, b, (((1,), (1,)), ((), ())), preferred_element_type=jn...]
    all_gather x1 -> x0, blocking collectives: 34.1 us -> none  [on_device(): lax.all_gather(weight_table(expert_ids, combine, n_experts), axes, axis=0...]
    convert_element_type x1 -> x0, other arithmetic: 4.33 us -> none  [on_device(): cotangent = (weight * g_all.astype(jnp.float32)).astype(jnp.bfloat16)]
    unnamed x19 -> x7, local copies, waits for them, and re-layouts: 1.71 us -> 5.89 us
  transfers between devices with their start and end apart: 4 -> 0, of which waited for: 4 -> 0; matrix products, arithmetic and copies ran while one was open for 15% -> 0% of each run, Pallas kernels for 0% -> 0%
where the time goes in v2:
time: 184 us
  Pallas kernels  170 us (92%)
  local copies, waits for them, and re-layouts  12.8 us (7%)
    pallas_call x1, Pallas kernels, fused_device(): pl.pallas_call(fused_kernel, out_shape=[jax.ShapeDtypeStruct((ROWS, width...  170 us
    unnamed x7, local copies, waits for them, and re-layouts  5.89 us

profile of v2, /device:TPU:14, one launch (start us, length us, event | category | flops | bytes accessed | tf_op | source)
XLA Modules:
  0.0 183.8 jit_solution(13779237142449962694)
XLA Ops:
  0.6 0.7 select_reduce_fusion
  1.4 0.1 copy.17
  1.4 0.1 copy.16
  1.5 1.0 concatenate.6
  2.6 0.7 pad.8.x_in
  3.3 1.7 pad.9.g_in
  5.0 169.7 %shard_map.110 = (bf16[64,2048]{1,0:T(8,128)(2,1)}, bf16[64,2048]{1,0:T(8,128)(2,1)}, bf16[1024,768]{1,0:T(8,128)(2,1)}, bf16[1024,768]{1,0:T(8,128)(2,1)}, bf16[768,1024]{1,0:T(8,128)(2,1)}) custom-call(bf16[64,2176]{1,0:T(8,128)(2,1)} %pad.8.x_in, bf16[64,2048]{1,0:T(8,128)(2,1)} %pad.9.g_in, bf16[2048,768]{1,0:T(8,128)(2,1)} %bitcast.6, ...), custom_call_target="tpu_custom_call" | custom-call | tf_op jit(solution)/shard_map/pallas_call | solution.py:265
  174.7 1.6 slice.6
  176.3 1.6 slice.7
  178.0 0.0 copy-start.1
  178.0 2.8 %copy.22 = bf16[1,1024,768]{2,1,0:T(8,128)(2,1)} copy(bf16[1,1024,768]{2,1,0:T(8,128)(2,1)} %bitcast.11) | data formatting | bytes 3145728
  180.7 0.0 copy-done.1
  180.7 0.0 copy-start
  180.7 1.1 copy.23
  181.9 0.8 copy-done
  182.7 1.1 copy.24
  (2 shorter events, 0.0 us)
Async XLA Ops:
  178.0 2.8 %copy-start.1 = (bf16[1024,768]{1,0:T(8,128)(2,1)S(1)}, bf16[1024,768]{1,0:T(8,128)(2,1)}, u32[]{:S(2)}) copy-start(bf16[1024,768]{1,0:T(8,128)(2,1)} %get-tuple-element.13) | copy-start | bytes 4718596
  180.7 2.0 %copy-start = (bf16[768,1024]{1,0:T(8,128)(2,1)S(1)}, bf16[768,1024]{1,0:T(8,128)(2,1)}, u32[]{:S(2)}) copy-start(bf16[768,1024]{1,0:T(8,128)(2,1)} %get-tuple-element.14) | copy-start | bytes 4718596

commit v3 on v2

--- a/solution.py
+++ b/solution.py
@@ -61,7 +61,7 @@
 
 
 def fused_kernel(x_in, g_in, wg_hbm, wu_hbm, wd_hbm, mixed_out, gt_out, gg_out, gu_out, gd_out,
-                 xs, gs, wg, wu, wd, hid, dg, du, part, s1, s2, s3,
+                 xs, gs, wg, wu, wd, hid, dg, du, xhalf, ghalf, place, rows, part, s1, s2, s3,
                  wsem, send, recv, rsend, rrecv):
     width = g_in.shape[1]
     half = width // 2
@@ -114,53 +114,87 @@
         along_y(a, 0).start()
         along_x(a, 0, 0).start()
         to_core(a, 0, 0, 0).start()
-    for a in (0, 1):
+    def from_z(a):
         for rz in (1, 3, 2):
             along_z(a, 4 - rz).wait_recv()
             along_y(a, rz).start()
             along_x(a, 0, rz).start()
             to_core(a, 0, 0, rz).start()
-    for a in (0, 1):
+
+    def from_y(a):
         for rz in (0, 1, 3, 2):
             along_y(a, rz).wait_recv()
             along_x(a, 1, rz).start()
             to_core(a, 0, 1, rz).start()
-    for load in loads:
-        load.wait()
+
+    def from_x(a, ry):
+        for rz in (0, 1, 3, 2):
+            along_x(a, ry, rz).wait_recv()
+            to_core(a, 1, ry, rz).start()
 
     lane = lax.broadcasted_iota(jnp.int32, (TILE, LANES), 1)
     mine = (lane < 48) & (lane % 16 == e)
-
-    def tile_pass(tile, own):
-        x = xs[tile, :, 0:width]
-        side = xs[tile, :, width:width + LANES].astype(jnp.float32)
-        weight = jnp.sum(jnp.where(mine, side, 0.0), axis=1, keepdims=True)
-        gate = dot_nn(x, wg[...])
-        upper = dot_nn(x, wu[...])
+    mine_half = pl.ds(pl.multiple_of(d * half, half), half)
+
+    def weight_of(side):
+        return jnp.sum(jnp.where(mine, side.astype(jnp.float32), 0.0), axis=1, keepdims=True)
+
+    def packed(rc):
+        return pl.ds(rc * LANES, LANES)
+
+    def forward(rx, ry):
+        chunk = 2 * rx + ry
+        for rz in range(4):
+            to_core(0, rx, ry, rz).wait_recv()
+        first = lax.broadcasted_iota(jnp.int32, (TILE, TILE), 0)
+        second = lax.broadcasted_iota(jnp.int32, (TILE, TILE), 1)
+        upto = ((second <= first) & (second // ROWS == first // ROWS)).astype(jnp.float32).astype(jnp.bfloat16)
+        base = (lax.broadcasted_iota(jnp.int32, (TILE, LANES), 0) // ROWS) * (LANES // 4)
+        slot = (lane - base + 1).astype(jnp.float32)
+        for rc in (0, 1):
+            tile = 2 * chunk + rc
+            weight = jnp.broadcast_to(weight_of(xs[tile, :, width:width + LANES]), (TILE, LANES))
+            chosen = jnp.where(weight > 0.0, 1.0, 0.0)
+            rank = dot_nn(upto, chosen.astype(jnp.bfloat16))
+            table = jnp.where(rank == slot, chosen, 0.0).astype(jnp.bfloat16)
+            place[tile] = table
+            rows[packed(rc), :] = dot_nn(table.T, xs[tile]).astype(jnp.bfloat16)
+        weight = weight_of(rows[:, width:width + LANES])
+        xhalf[chunk] = rows[:, mine_half]
+        gate = dot_nn(rows[:, 0:width], wg[...])
+        upper = dot_nn(rows[:, 0:width], wu[...])
         sigma = jax.nn.sigmoid(gate)
-        silu = gate * sigma
-        hidden = (silu * upper * weight).astype(jnp.bfloat16)
-        hid[tile] = hidden
-        d_hidden = weight * dot_nt(gs[tile], wd[...])
-        d_gate = (d_hidden * upper * sigma * (1.0 + gate * (1.0 - sigma))).astype(jnp.bfloat16)
-        d_upper = (d_hidden * silu).astype(jnp.bfloat16)
-        dg[tile] = d_gate
-        du[tile] = d_upper
-        if own:
-            part[0, tile] = dot_nn(hidden, wd[...]).astype(jnp.bfloat16)
-            part[1, tile] = (dot_nt(d_gate, wg[...]) + dot_nt(d_upper, wu[...])).astype(jnp.bfloat16)
-
-    def chunk(rx, ry):
-        for a in (0, 1):
-            for rz in range(4):
-                to_core(a, rx, ry, rz).wait_recv()
-        first = 4 * rx + 2 * ry
-
-        def step(i, carry):
-            tile_pass(first + i, rx == 0)
-            return carry
-
-        lax.fori_loop(0, 2, step, 0)
+        silu = gate * sigma * weight
+        hidden = (silu * upper).astype(jnp.bfloat16)
+        hid[chunk] = hidden
+        dg[chunk] = (weight * upper * sigma * (1.0 + gate * (1.0 - sigma))).astype(jnp.bfloat16)
+        du[chunk] = silu.astype(jnp.bfloat16)
+        if rx == 0:
+            out = dot_nn(hidden, wd[...]).astype(jnp.bfloat16)
+            for rc in (0, 1):
+                part[0, 2 * chunk + rc] = dot_nn(
+                    place[2 * chunk + rc], out[rc * LANES:(rc + 1) * LANES]).astype(jnp.bfloat16)
+            sum_core(0, ry).start()
+
+    def backward(rx, ry):
+        chunk = 2 * rx + ry
+        for rz in range(4):
+            to_core(1, rx, ry, rz).wait_recv()
+        for rc in (0, 1):
+            tile = 2 * chunk + rc
+            rows[packed(rc), 0:width] = dot_nn(place[tile].T, gs[tile]).astype(jnp.bfloat16)
+        ghalf[chunk] = rows[:, mine_half]
+        d_hidden = dot_nt(rows[:, 0:width], wd[...])
+        d_gate = (d_hidden * dg[chunk].astype(jnp.float32)).astype(jnp.bfloat16)
+        d_upper = (d_hidden * du[chunk].astype(jnp.float32)).astype(jnp.bfloat16)
+        dg[chunk] = d_gate
+        du[chunk] = d_upper
+        if rx == 0:
+            out = (dot_nt(d_gate, wg[...]) + dot_nt(d_upper, wu[...])).astype(jnp.bfloat16)
+            for rc in (0, 1):
+                part[1, 2 * chunk + rc] = dot_nn(
+                    place[2 * chunk + rc], out[rc * LANES:(rc + 1) * LANES]).astype(jnp.bfloat16)
+            sum_core(1, ry).start()
 
     def rcopy(src, dst, a, sem, device):
         return pltpu.make_async_remote_copy(
@@ -180,52 +214,60 @@
         total = part[a, tile].astype(jnp.float32) + other.astype(jnp.float32)
         part[a, tile] = total.astype(jnp.bfloat16)
 
-    def from_x(ry):
-        for a in (0, 1):
-            for rz in (0, 1, 3, 2):
-                along_x(a, ry, rz).wait_recv()
-                to_core(a, 1, ry, rz).start()
-
-    chunk(0, 0)
-    for a in (0, 1):
-        sum_core(a, 0).start()
-    chunk(0, 1)
-    for a in (0, 1):
-        sum_core(a, 1).start()
-    from_x(0)
-    for a in (0, 1):
+    def sums_over_core(a):
         sum_core(a, 1).wait_recv()
         add(a, 2, s1[a, 1])
         sum_y(a).start()
         sum_core(a, 0).wait_recv()
         add(a, 0, s1[a, 0])
-    chunk(1, 0)
-    for a in (0, 1):
+
+    def sums_over_y(a):
         sum_y(a).wait_recv()
         add(a, 0, s2[a])
         for rz in (1, 2, 3):
             sum_z(a, rz).start()
-    from_x(1)
-    chunk(1, 1)
+
+    from_z(0)
+    for load in loads:
+        load.wait()
+    forward(0, 0)
+    from_y(0)
+    forward(0, 1)
+    from_x(0, 0)
+    sums_over_core(0)
+    forward(1, 0)
+    from_z(1)
+    backward(0, 0)
+    from_y(1)
+    sums_over_y(0)
+    from_x(0, 1)
+    backward(0, 1)
+    forward(1, 1)
+    sums_over_core(1)
+    from_x(1, 0)
+    backward(1, 0)
+    sums_over_y(1)
+    from_x(1, 1)
+    backward(1, 1)
+
+    packed_rows = 4 * TILE
 
     def grads_in(j, carry):
-        columns = pl.ds(pl.multiple_of(d * half + j * TILE, TILE), TILE)
-        xt = xs[:, :, columns].reshape(8 * TILE, TILE).T
-        rows = pl.ds(pl.multiple_of(j * TILE, TILE), TILE)
-        gg_out[rows, :] = dot_nn(xt, dg[...].reshape(8 * TILE, -1)).astype(jnp.bfloat16)
-        gu_out[rows, :] = dot_nn(xt, du[...].reshape(8 * TILE, -1)).astype(jnp.bfloat16)
+        block = pl.ds(pl.multiple_of(j * 512, 512), 512)
+        xt = xhalf[:, :, block].reshape(packed_rows, 512).T
+        gg_out[block, :] = dot_nn(xt, dg[...].reshape(packed_rows, -1)).astype(jnp.bfloat16)
+        gu_out[block, :] = dot_nn(xt, du[...].reshape(packed_rows, -1)).astype(jnp.bfloat16)
         return carry
 
-    lax.fori_loop(0, half // TILE, grads_in, 0)
+    lax.fori_loop(0, half // 512, grads_in, 0)
 
     def grads_down(j, carry):
-        columns = pl.ds(pl.multiple_of(j * TILE, TILE), TILE)
-        ht = hid[:, :, columns].reshape(8 * TILE, TILE).T
-        mine_half = pl.ds(pl.multiple_of(d * half, half), half)
-        gd_out[columns, :] = dot_nn(ht, gs[:, :, mine_half].reshape(8 * TILE, half)).astype(jnp.bfloat16)
+        block = pl.ds(pl.multiple_of(j * 384, 384), 384)
+        ht = hid[:, :, block].reshape(packed_rows, 384).T
+        gd_out[block, :] = dot_nn(ht, ghalf[...].reshape(packed_rows, half)).astype(jnp.bfloat16)
         return carry
 
-    lax.fori_loop(0, hid.shape[2] // TILE, grads_down, 0)
+    lax.fori_loop(0, hid.shape[2] // 384, grads_down, 0)
 
     for a, out in ((0, mixed_out), (1, gt_out)):
         total = part[a, 0, 0:ROWS].astype(jnp.float32)
@@ -279,9 +321,13 @@
             pltpu.VMEM((width, hidden), bf16),
             pltpu.VMEM((width, hidden), bf16),
             pltpu.VMEM((hidden, width), bf16),
-            pltpu.VMEM((8, TILE, hidden), bf16),
-            pltpu.VMEM((8, TILE, hidden), bf16),
-            pltpu.VMEM((8, TILE, hidden), bf16),
+            pltpu.VMEM((4, TILE, hidden), bf16),
+            pltpu.VMEM((4, TILE, hidden), bf16),
+            pltpu.VMEM((4, TILE, hidden), bf16),
+            pltpu.VMEM((4, TILE, width // 2), bf16),
+            pltpu.VMEM((4, TILE, width // 2), bf16),
+            pltpu.VMEM((8, TILE, LANES), bf16),
+            pltpu.VMEM((TILE, width + LANES), bf16),
             pltpu.VMEM((2, 4, TILE, width), bf16),
             pltpu.VMEM((2, 2, TILE, width), bf16),
             pltpu.VMEM((2, TILE, width), bf16),

time: 184 us -> 172 us (0.935); the launches traced: 184 us -> 169 us
  Pallas kernels: 170 us -> 155 us
    pallas_call x1, Pallas kernels: 170 us -> 155 us  [fused_device(): pl.pallas_call(fused_kernel, out_shape=[jax.ShapeDtypeStruct((ROWS, width...]
where the time goes in v3:
time: 172 us; the launch traced here: 169 us
  Pallas kernels  155 us (90%)
  local copies, waits for them, and re-layouts  12.8 us (7%)
    pallas_call x1, Pallas kernels, fused_device(): pl.pallas_call(fused_kernel, out_shape=[jax.ShapeDtypeStruct((ROWS, width...  155 us
    unnamed x7, local copies, waits for them, and re-layouts  5.89 us

profile of v3, /device:TPU:14, one launch (start us, length us, event | category | flops | bytes accessed | tf_op | source)
XLA Modules:
  0.0 169.3 jit_solution(11963625164059913627)
XLA Ops:
  0.6 0.7 select_reduce_fusion
  1.4 0.1 copy.17
  1.4 0.1 copy.16
  1.5 1.0 concatenate.6
  2.6 0.7 pad.8.x_in
  3.3 1.7 pad.9.g_in
  5.0 155.2 %shard_map.110 = (bf16[64,2048]{1,0:T(8,128)(2,1)}, bf16[64,2048]{1,0:T(8,128)(2,1)}, bf16[1024,768]{1,0:T(8,128)(2,1)}, bf16[1024,768]{1,0:T(8,128)(2,1)}, bf16[768,1024]{1,0:T(8,128)(2,1)}) custom-call(bf16[64,2176]{1,0:T(8,128)(2,1)} %pad.8.x_in, bf16[64,2048]{1,0:T(8,128)(2,1)} %pad.9.g_in, bf16[2048,768]{1,0:T(8,128)(2,1)} %bitcast.6, ...), custom_call_target="tpu_custom_call" | custom-call | tf_op jit(solution)/shard_map/pallas_call | solution.py:307
  160.1 1.6 slice.6
  161.8 1.6 slice.7
  163.4 0.0 copy-start.1
  163.4 2.8 %copy.22 = bf16[1,1024,768]{2,1,0:T(8,128)(2,1)} copy(bf16[1,1024,768]{2,1,0:T(8,128)(2,1)} %bitcast.11) | data formatting | bytes 3145728
  166.2 0.0 copy-done.1
  166.2 0.0 copy-start
  166.2 1.1 copy.23
  167.3 0.8 copy-done
  168.2 1.1 copy.24
  (2 shorter events, 0.0 us)
Async XLA Ops:
  163.4 2.8 %copy-start.1 = (bf16[1024,768]{1,0:T(8,128)(2,1)S(1)}, bf16[1024,768]{1,0:T(8,128)(2,1)}, u32[]{:S(2)}) copy-start(bf16[1024,768]{1,0:T(8,128)(2,1)} %get-tuple-element.13) | copy-start | bytes 4718596
  166.2 2.0 %copy-start = (bf16[768,1024]{1,0:T(8,128)(2,1)S(1)}, bf16[768,1024]{1,0:T(8,128)(2,1)}, u32[]{:S(2)}) copy-start(bf16[768,1024]{1,0:T(8,128)(2,1)} %get-tuple-element.14) | copy-start | bytes 4718596

commit v4 on v3

--- a/solution.py
+++ b/solution.py
@@ -54,13 +54,14 @@
     return mixed, grad_tokens, grad_g[None], grad_u[None], grad_d[None]
 
 
-ROWS = 64
+ROWS = (64, 48)
+TAIL = 8
 TILE = 256
 Z, XD, YD, SD = 0, 3, 7, 15
 LANES = 128
 
 
-def fused_kernel(x_in, g_in, wg_hbm, wu_hbm, wd_hbm, mixed_out, gt_out, gg_out, gu_out, gd_out,
+def fused_kernel(x_in, side_in, g_in, wg_hbm, wu_hbm, wd_hbm, mixed_out, gt_out, gg_out, gu_out, gd_out,
                  xs, gs, wg, wu, wd, hid, dg, du, xhalf, ghalf, place, rows, part, s1, s2, s3,
                  wsem, send, recv, rsend, rrecv):
     width = g_in.shape[1]
@@ -82,14 +83,17 @@
     barrier = pltpu.get_barrier_semaphore()
     for partner in partners:
         pl.semaphore_signal(barrier, inc=1, device_id=partner, device_id_type=pl.DeviceIdType.MESH)
-    xs[0, 0:ROWS, :] = x_in[...]
-    gs[0, 0:ROWS, :] = g_in[...]
+    tok = x_in.shape[0]
+    xs[0, 0:ROWS[0], 0:width] = jnp.concatenate(
+        [x_in[...].astype(jnp.float32), g_in[ROWS[1]:tok, :].astype(jnp.float32)], axis=0).astype(jnp.bfloat16)
+    xs[0, 0:ROWS[0], width:width + LANES] = side_in[...]
+    gs[0, 0:ROWS[1], :] = g_in[0:ROWS[1], :]
     pl.semaphore_wait(barrier, len(partners))
 
     slots = (xs, gs)
 
     def shard(a, tile, rz):
-        return slots[a].at[tile, pl.ds(rz * ROWS, ROWS)]
+        return slots[a].at[tile, pl.ds(rz * ROWS[a], ROWS[a])]
 
     def copy(a, src, dst, sem, device):
         return pltpu.make_async_remote_copy(
@@ -133,68 +137,76 @@
             to_core(a, 1, ry, rz).start()
 
     lane = lax.broadcasted_iota(jnp.int32, (TILE, LANES), 1)
-    mine = (lane < 48) & (lane % 16 == e)
     mine_half = pl.ds(pl.multiple_of(d * half, half), half)
 
     def weight_of(side):
+        at = lax.broadcasted_iota(jnp.int32, side.shape, 1)
+        mine = (at < 48) & (at % 16 == e)
         return jnp.sum(jnp.where(mine, side.astype(jnp.float32), 0.0), axis=1, keepdims=True)
 
-    def packed(rc):
-        return pl.ds(rc * LANES, LANES)
-
-    def forward(rx, ry):
-        chunk = 2 * rx + ry
-        for rz in range(4):
-            to_core(0, rx, ry, rz).wait_recv()
+    def packed(i):
+        return pl.ds(i * LANES, LANES)
+
+    def forward(rx):
         first = lax.broadcasted_iota(jnp.int32, (TILE, TILE), 0)
         second = lax.broadcasted_iota(jnp.int32, (TILE, TILE), 1)
-        upto = ((second <= first) & (second // ROWS == first // ROWS)).astype(jnp.float32).astype(jnp.bfloat16)
-        base = (lax.broadcasted_iota(jnp.int32, (TILE, LANES), 0) // ROWS) * (LANES // 4)
+        upto = ((second <= first) & (second // 64 == first // 64)).astype(jnp.float32).astype(jnp.bfloat16)
+        base = (lax.broadcasted_iota(jnp.int32, (TILE, LANES), 0) // 64) * (LANES // 4)
         slot = (lane - base + 1).astype(jnp.float32)
-        for rc in (0, 1):
-            tile = 2 * chunk + rc
+        for i in range(4):
+            for rz in range(4 * (i % 2)):
+                to_core(0, rx, i // 2, rz).wait_recv()
+            tile = 4 * rx + i
             weight = jnp.broadcast_to(weight_of(xs[tile, :, width:width + LANES]), (TILE, LANES))
             chosen = jnp.where(weight > 0.0, 1.0, 0.0)
             rank = dot_nn(upto, chosen.astype(jnp.bfloat16))
             table = jnp.where(rank == slot, chosen, 0.0).astype(jnp.bfloat16)
             place[tile] = table
-            rows[packed(rc), :] = dot_nn(table.T, xs[tile]).astype(jnp.bfloat16)
+            rows[packed(i), :] = dot_nn(table.T, xs[tile]).astype(jnp.bfloat16)
         weight = weight_of(rows[:, width:width + LANES])
-        xhalf[chunk] = rows[:, mine_half]
-        gate = dot_nn(rows[:, 0:width], wg[...])
-        upper = dot_nn(rows[:, 0:width], wu[...])
-        sigma = jax.nn.sigmoid(gate)
-        silu = gate * sigma * weight
-        hidden = (silu * upper).astype(jnp.bfloat16)
-        hid[chunk] = hidden
-        dg[chunk] = (weight * upper * sigma * (1.0 + gate * (1.0 - sigma))).astype(jnp.bfloat16)
-        du[chunk] = silu.astype(jnp.bfloat16)
+        xhalf[rx] = rows[:, mine_half]
+        for h in range(hid.shape[2] // TILE):
+            cols = pl.ds(h * TILE, TILE)
+            gate = dot_nn(rows[:, 0:width], wg[:, cols])
+            upper = dot_nn(rows[:, 0:width], wu[:, cols])
+            sigma = jax.nn.sigmoid(gate)
+            silu = gate * sigma * weight
+            hid[rx, :, cols] = (silu * upper).astype(jnp.bfloat16)
+            dg[rx, :, cols] = (weight * upper * sigma * (1.0 + gate * (1.0 - sigma))).astype(jnp.bfloat16)
+            du[rx, :, cols] = silu.astype(jnp.bfloat16)
         if rx == 0:
-            out = dot_nn(hidden, wd[...]).astype(jnp.bfloat16)
-            for rc in (0, 1):
-                part[0, 2 * chunk + rc] = dot_nn(
-                    place[2 * chunk + rc], out[rc * LANES:(rc + 1) * LANES]).astype(jnp.bfloat16)
-            sum_core(0, ry).start()
-
-    def backward(rx, ry):
-        chunk = 2 * rx + ry
-        for rz in range(4):
-            to_core(1, rx, ry, rz).wait_recv()
-        for rc in (0, 1):
-            tile = 2 * chunk + rc
-            rows[packed(rc), 0:width] = dot_nn(place[tile].T, gs[tile]).astype(jnp.bfloat16)
-        ghalf[chunk] = rows[:, mine_half]
-        d_hidden = dot_nt(rows[:, 0:width], wd[...])
-        d_gate = (d_hidden * dg[chunk].astype(jnp.float32)).astype(jnp.bfloat16)
-        d_upper = (d_hidden * du[chunk].astype(jnp.float32)).astype(jnp.bfloat16)
-        dg[chunk] = d_gate
-        du[chunk] = d_upper
+            spread(0, lambda cols: dot_nn(hid[0], wd[:, cols]))
+
+    def spread(a, product):
+        for n in range(width // 512):
+            cols = pl.ds(n * 512, 512)
+            out = product(cols).astype(jnp.bfloat16)
+            for i in range(4):
+                part[a, i, :, cols] = dot_nn(place[i], out[i * LANES:(i + 1) * LANES]).astype(jnp.bfloat16)
+        for ry in (0, 1):
+            sum_core(a, ry).start()
+
+    def backward(rx):
+        for i in range(4):
+            for rz in range(4 * (i % 2)):
+                to_core(1, rx, i // 2, rz).wait_recv()
+            tile = 4 * rx + i
+            table = place[tile].astype(jnp.float32)
+            blank = jnp.zeros((TAIL, LANES), jnp.float32)
+            heads = [table[64 * rz:64 * rz + 48] for rz in range(4)]
+            tails = [t for rz in range(4) for t in (blank, table[64 * rz + 48:64 * rz + 56])]
+            table = jnp.concatenate(heads + tails, axis=0).astype(jnp.bfloat16)
+            grads = jnp.concatenate(
+                [gs[tile]] + [xs[tile, 64 * rz + 48:64 * rz + 64, 0:width] for rz in range(4)], axis=0)
+            rows[packed(i), 0:width] = dot_nn(table.T, grads).astype(jnp.bfloat16)
+        ghalf[rx] = rows[:, mine_half]
+        for h in range(hid.shape[2] // TILE):
+            cols = pl.ds(h * TILE, TILE)
+            d_hidden = dot_nt(rows[:, 0:width], wd[cols, :])
+            dg[rx, :, cols] = (d_hidden * dg[rx, :, cols].astype(jnp.float32)).astype(jnp.bfloat16)
+            du[rx, :, cols] = (d_hidden * du[rx, :, cols].astype(jnp.float32)).astype(jnp.bfloat16)
         if rx == 0:
-            out = (dot_nt(d_gate, wg[...]) + dot_nt(d_upper, wu[...])).astype(jnp.bfloat16)
-            for rc in (0, 1):
-                part[1, 2 * chunk + rc] = dot_nn(
-                    place[2 * chunk + rc], out[rc * LANES:(rc + 1) * LANES]).astype(jnp.bfloat16)
-            sum_core(1, ry).start()
+            spread(1, lambda cols: dot_nt(dg[0], wg[cols, :]) + dot_nt(du[0], wu[cols, :]))
 
     def rcopy(src, dst, a, sem, device):
         return pltpu.make_async_remote_copy(
@@ -208,7 +220,7 @@
         return rcopy(part.at[a, 2], s2.at[a], a, 2, across_y)
 
     def sum_z(a, rz):
-        return rcopy(part.at[a, 0, pl.ds(rz * ROWS, ROWS)], s3.at[a, 3 - rz], a, 2 + rz, peer(0, 0, rz, 0))
+        return rcopy(part.at[a, 0, pl.ds(rz * ROWS[0], ROWS[0])], s3.at[a, 3 - rz], a, 2 + rz, peer(0, 0, rz, 0))
 
     def add(a, tile, other):
         total = part[a, tile].astype(jnp.float32) + other.astype(jnp.float32)
@@ -228,27 +240,23 @@
             sum_z(a, rz).start()
 
     from_z(0)
+    from_y(0)
     for load in loads:
         load.wait()
-    forward(0, 0)
-    from_y(0)
-    forward(0, 1)
+    forward(0)
     from_x(0, 0)
+    from_z(1)
     sums_over_core(0)
-    forward(1, 0)
-    from_z(1)
-    backward(0, 0)
     from_y(1)
+    from_x(0, 1)
+    backward(0)
     sums_over_y(0)
-    from_x(0, 1)
-    backward(0, 1)
-    forward(1, 1)
+    from_x(1, 0)
+    forward(1)
     sums_over_core(1)
-    from_x(1, 0)
-    backward(1, 0)
+    from_x(1, 1)
     sums_over_y(1)
-    from_x(1, 1)
-    backward(1, 1)
+    backward(1)
 
     packed_rows = 4 * TILE
 
@@ -270,12 +278,12 @@
     lax.fori_loop(0, hid.shape[2] // 384, grads_down, 0)
 
     for a, out in ((0, mixed_out), (1, gt_out)):
-        total = part[a, 0, 0:ROWS].astype(jnp.float32)
+        total = part[a, 0, 0:ROWS[0]].astype(jnp.float32)
         for rz in (1, 2, 3):
             sum_z(a, rz).wait_recv()
         for i in range(3):
             total = total + s3[a, i].astype(jnp.float32)
-        out[...] = total.astype(jnp.bfloat16)
+        out[...] = total[0:tok].astype(jnp.bfloat16)
 
     for a in (0, 1):
         for rz in (1, 2, 3):
@@ -299,39 +307,38 @@
     high = lax.reduce_precision(table, 8, 7)
     mid = lax.reduce_precision(table - high, 8, 7)
     side = jnp.concatenate([high, mid, table - high - mid], axis=1).astype(jnp.bfloat16)
-    x = jnp.pad(jnp.concatenate([tokens, side], axis=1), ((0, ROWS - tok), (0, LANES - side.shape[1])))
-    g = jnp.pad(grad_out, ((0, ROWS - tok), (0, 0)))
+    side = jnp.pad(side, ((0, ROWS[0] - tok), (0, LANES - side.shape[1])))
     bf16 = jnp.bfloat16
     vmem = pl.BlockSpec(memory_space=pltpu.VMEM)
     hbm = pl.BlockSpec(memory_space=pl.ANY)
     mixed, grad_tokens, grad_g, grad_u, grad_d = pl.pallas_call(
         fused_kernel,
         out_shape=[
-            jax.ShapeDtypeStruct((ROWS, width), bf16),
-            jax.ShapeDtypeStruct((ROWS, width), bf16),
+            jax.ShapeDtypeStruct((tok, width), bf16),
+            jax.ShapeDtypeStruct((tok, width), bf16),
             jax.ShapeDtypeStruct((width // 2, hidden), bf16),
             jax.ShapeDtypeStruct((width // 2, hidden), bf16),
             jax.ShapeDtypeStruct((hidden, width // 2), bf16),
         ],
-        in_specs=[vmem, vmem, hbm, hbm, hbm],
+        in_specs=[vmem, vmem, vmem, hbm, hbm, hbm],
         out_specs=[vmem] * 5,
         scratch_shapes=[
             pltpu.VMEM((8, TILE, width + LANES), bf16),
-            pltpu.VMEM((8, TILE, width), bf16),
+            pltpu.VMEM((8, 4 * ROWS[1], width), bf16),
             pltpu.VMEM((width, hidden), bf16),
             pltpu.VMEM((width, hidden), bf16),
             pltpu.VMEM((hidden, width), bf16),
-            pltpu.VMEM((4, TILE, hidden), bf16),
-            pltpu.VMEM((4, TILE, hidden), bf16),
-            pltpu.VMEM((4, TILE, hidden), bf16),
-            pltpu.VMEM((4, TILE, width // 2), bf16),
-            pltpu.VMEM((4, TILE, width // 2), bf16),
+            pltpu.VMEM((2, 2 * TILE, hidden), bf16),
+            pltpu.VMEM((2, 2 * TILE, hidden), bf16),
+            pltpu.VMEM((2, 2 * TILE, hidden), bf16),
+            pltpu.VMEM((2, 2 * TILE, width // 2), bf16),
+            pltpu.VMEM((2, 2 * TILE, width // 2), bf16),
             pltpu.VMEM((8, TILE, LANES), bf16),
-            pltpu.VMEM((TILE, width + LANES), bf16),
+            pltpu.VMEM((2 * TILE, width + LANES), bf16),
             pltpu.VMEM((2, 4, TILE, width), bf16),
             pltpu.VMEM((2, 2, TILE, width), bf16),
             pltpu.VMEM((2, TILE, width), bf16),
-            pltpu.VMEM((2, 3, ROWS, width), bf16),
+            pltpu.VMEM((2, 3, ROWS[0], width), bf16),
             pltpu.SemaphoreType.DMA((3,)),
             pltpu.SemaphoreType.DMA((2, 31)),
             pltpu.SemaphoreType.DMA((2, 31)),
@@ -340,8 +347,8 @@
         ],
         compiler_params=pltpu.CompilerParams(
             collective_id=0, has_side_effects=True, vmem_limit_bytes=63 * 1024 * 1024),
-    )(x, g, w_gate[0], w_up[0], w_down[0])
-    return mixed[:tok], grad_tokens[:tok], grad_g[None], grad_u[None], grad_d[None]
+    )(tokens, side, grad_out, w_gate[0], w_up[0], w_down[0])
+    return mixed, grad_tokens, grad_g[None], grad_u[None], grad_d[None]
 
 
 def solution(mesh):

time: 172 us -> 161 us (0.936)
  Pallas kernels: 155 us -> 146 us
  local copies, waits for them, and re-layouts: 12.8 us -> 9.33 us
    pallas_call x1, Pallas kernels: 155 us -> 146 us  [fused_device(): pl.pallas_call(fused_kernel, out_shape=[jax.ShapeDtypeStruct((tok, width)...]
    unnamed x7 -> x9, local copies, waits for them, and re-layouts: 5.89 us -> 9.17 us
    slice x2 -> x0, local copies, waits for them, and re-layouts: 3.28 us -> none  [the longest x1 1.64 us: fused_device(): mixed[:tok]]
    pad x2 -> x0, local copies, waits for them, and re-layouts: 2.39 us -> none  [the longest x1 1.66 us: fused_device(): g = jnp.pad(grad_out, ((0, ROWS - tok), (0, 0)))]
where the time goes in v4:
time: 161 us; the launch traced here: 158 us
  Pallas kernels  146 us (91%)
  local copies, waits for them, and re-layouts  9.33 us (6%)
    pallas_call x1, Pallas kernels, fused_device(): pl.pallas_call(fused_kernel, out_shape=[jax.ShapeDtypeStruct((tok, width)...  146 us
    unnamed x9, local copies, waits for them, and re-layouts  9.17 us

profile of v4, /device:TPU:14, one launch (start us, length us, event | category | flops | bytes accessed | tf_op | source)
XLA Modules:
  0.0 157.8 jit_solution(14632468092684492756)
XLA Ops:
  0.6 0.7 select_reduce_fusion
  1.4 0.1 copy.17
  1.4 0.1 copy.16
  1.5 0.7 fusion.9.side_in
  2.2 146.3 %shard_map.110 = (bf16[56,2048]{1,0:T(8,128)(2,1)}, bf16[56,2048]{1,0:T(8,128)(2,1)}, bf16[1024,768]{1,0:T(8,128)(2,1)}, bf16[1024,768]{1,0:T(8,128)(2,1)}, bf16[768,1024]{1,0:T(8,128)(2,1)}) custom-call(bf16[56,2048]{1,0:T(8,128)(2,1)} %x_in.1, bf16[64,128]{1,0:T(8,128)(2,1)} %fusion.9.side_in, bf16[56,2048]{1,0:T(8,128)(2,1)} %g_in.1, ...), custom_call_target="tpu_custom_call" | custom-call | tf_op jit(solution)/shard_map/pallas_call | solution.py:314
  148.6 1.6 %copy.24 = bf16[56,2048]{1,0:T(8,128)(2,1)} copy(bf16[56,2048]{1,0:T(8,128)(2,1)} %get-tuple-element.23) | data formatting | bytes 458752
  150.2 1.6 %copy.25 = bf16[56,2048]{1,0:T(8,128)(2,1)} copy(bf16[56,2048]{1,0:T(8,128)(2,1)} %get-tuple-element.24) | data formatting | bytes 458752
  151.9 0.0 copy-start.1
  151.9 2.8 %copy.26 = bf16[1,1024,768]{2,1,0:T(8,128)(2,1)} copy(bf16[1,1024,768]{2,1,0:T(8,128)(2,1)} %bitcast.11) | data formatting | bytes 3145728
  154.6 0.0 copy-done.1
  154.6 0.0 copy-start
  154.7 1.1 copy.27
  155.8 0.8 copy-done
  156.6 1.1 copy.28
  (2 shorter events, 0.0 us)
Async XLA Ops:
  151.9 2.8 %copy-start.1 = (bf16[1024,768]{1,0:T(8,128)(2,1)S(1)}, bf16[1024,768]{1,0:T(8,128)(2,1)}, u32[]{:S(2)}) copy-start(bf16[1024,768]{1,0:T(8,128)(2,1)} %get-tuple-element.13) | copy-start | bytes 4718596
  154.6 2.0 %copy-start = (bf16[768,1024]{1,0:T(8,128)(2,1)S(1)}, bf16[768,1024]{1,0:T(8,128)(2,1)}, u32[]{:S(2)}) copy-start(bf16[768,1024]{1,0:T(8,128)(2,1)} %get-tuple-element.14) | copy-start | bytes 4718596

commit v5 on v4

--- a/solution.py
+++ b/solution.py
@@ -244,38 +244,43 @@
     for load in loads:
         load.wait()
     forward(0)
+    from_z(1)
     from_x(0, 0)
-    from_z(1)
     sums_over_core(0)
     from_y(1)
+    backward(0)
     from_x(0, 1)
-    backward(0)
+    sums_over_core(1)
     sums_over_y(0)
+    forward(1)
     from_x(1, 0)
-    forward(1)
-    sums_over_core(1)
+    sums_over_y(1)
+
+    def weight_grads(rx):
+        def store(out, block, product):
+            if rx == 1:
+                product = product + out[block, :].astype(jnp.float32)
+            out[block, :] = product.astype(jnp.bfloat16)
+
+        def grads_in(j, carry):
+            block = pl.ds(pl.multiple_of(j * 512, 512), 512)
+            xt = xhalf[rx, :, block].T
+            store(gg_out, block, dot_nn(xt, dg[rx]))
+            store(gu_out, block, dot_nn(xt, du[rx]))
+            return carry
+
+        def grads_down(j, carry):
+            block = pl.ds(pl.multiple_of(j * 384, 384), 384)
+            store(gd_out, block, dot_nn(hid[rx, :, block].T, ghalf[rx]))
+            return carry
+
+        lax.fori_loop(0, half // 512, grads_in, 0)
+        lax.fori_loop(0, hid.shape[2] // 384, grads_down, 0)
+
+    weight_grads(0)
     from_x(1, 1)
-    sums_over_y(1)
     backward(1)
-
-    packed_rows = 4 * TILE
-
-    def grads_in(j, carry):
-        block = pl.ds(pl.multiple_of(j * 512, 512), 512)
-        xt = xhalf[:, :, block].reshape(packed_rows, 512).T
-        gg_out[block, :] = dot_nn(xt, dg[...].reshape(packed_rows, -1)).astype(jnp.bfloat16)
-        gu_out[block, :] = dot_nn(xt, du[...].reshape(packed_rows, -1)).astype(jnp.bfloat16)
-        return carry
-
-    lax.fori_loop(0, half // 512, grads_in, 0)
-
-    def grads_down(j, carry):
-        block = pl.ds(pl.multiple_of(j * 384, 384), 384)
-        ht = hid[:, :, block].reshape(packed_rows, 384).T
-        gd_out[block, :] = dot_nn(ht, ghalf[...].reshape(packed_rows, half)).astype(jnp.bfloat16)
-        return carry
-
-    lax.fori_loop(0, hid.shape[2] // 384, grads_down, 0)
+    weight_grads(1)
 
     for a, out in ((0, mixed_out), (1, gt_out)):
         total = part[a, 0, 0:ROWS[0]].astype(jnp.float32)

time: 161 us -> 153 us (0.950)
  Pallas kernels: 146 us -> 140 us
    pallas_call x1, Pallas kernels: 146 us -> 140 us  [fused_device(): pl.pallas_call(fused_kernel, out_shape=[jax.ShapeDtypeStruct((tok, width)...]
where the time goes in v5:
time: 153 us; the launch traced here: 151 us
  Pallas kernels  140 us (92%)
  local copies, waits for them, and re-layouts  9.33 us (6%)
    pallas_call x1, Pallas kernels, fused_device(): pl.pallas_call(fused_kernel, out_shape=[jax.ShapeDtypeStruct((tok, width)...  140 us
    unnamed x9, local copies, waits for them, and re-layouts  9.17 us

profile of v5, /device:TPU:14, one launch (start us, length us, event | category | flops | bytes accessed | tf_op | source)
XLA Modules:
  0.0 151.0 jit_solution(1579921141154630634)
XLA Ops:
  0.6 0.7 select_reduce_fusion
  1.4 0.1 copy.17
  1.4 0.1 copy.16
  1.5 0.7 fusion.9.side_in
  2.2 139.6 %shard_map.110 = (bf16[56,2048]{1,0:T(8,128)(2,1)}, bf16[56,2048]{1,0:T(8,128)(2,1)}, bf16[1024,768]{1,0:T(8,128)(2,1)}, bf16[1024,768]{1,0:T(8,128)(2,1)}, bf16[768,1024]{1,0:T(8,128)(2,1)}) custom-call(bf16[56,2048]{1,0:T(8,128)(2,1)} %x_in.1, bf16[64,128]{1,0:T(8,128)(2,1)} %fusion.9.side_in, bf16[56,2048]{1,0:T(8,128)(2,1)} %g_in.1, ...), custom_call_target="tpu_custom_call" | custom-call | tf_op jit(solution)/shard_map/pallas_call | solution.py:319
  141.9 1.6 %copy.24 = bf16[56,2048]{1,0:T(8,128)(2,1)} copy(bf16[56,2048]{1,0:T(8,128)(2,1)} %get-tuple-element.23) | data formatting | bytes 458752
  143.5 1.6 %copy.25 = bf16[56,2048]{1,0:T(8,128)(2,1)} copy(bf16[56,2048]{1,0:T(8,128)(2,1)} %get-tuple-element.24) | data formatting | bytes 458752
  145.1 0.0 copy-start.1
  145.1 2.8 %copy.26 = bf16[1,1024,768]{2,1,0:T(8,128)(2,1)} copy(bf16[1,1024,768]{2,1,0:T(8,128)(2,1)} %bitcast.11) | data formatting | bytes 3145728
  147.9 0.0 copy-done.1
  147.9 0.0 copy-start
  147.9 1.1 copy.27
  149.1 0.8 copy-done
  149.9 1.1 copy.28
  (2 shorter events, 0.0 us)
Async XLA Ops:
  145.1 2.8 %copy-start.1 = (bf16[1024,768]{1,0:T(8,128)(2,1)S(1)}, bf16[1024,768]{1,0:T(8,128)(2,1)}, u32[]{:S(2)}) copy-start(bf16[1024,768]{1,0:T(8,128)(2,1)} %get-tuple-element.13) | copy-start | bytes 4718596
  147.9 2.0 %copy-start = (bf16[768,1024]{1,0:T(8,128)(2,1)S(1)}, bf16[768,1024]{1,0:T(8,128)(2,1)}, u32[]{:S(2)}) copy-start(bf16[768,1024]{1,0:T(8,128)(2,1)} %get-tuple-element.14) | copy-start | bytes 4718596
